TPU v7x, 128 devices: a whole 4x4x4 slice. The times are simulated.
128 devices in a mesh: var: 32 (over x, y, core), grp: 4 (over z).
Axes of the slice: x: 4, y: 4, z: 4, core: 2. Of those that a mesh axis runs over, the one named last changes fastest.
Arguments:
- series: bfloat16 [131072, 2048], P(('var', 'grp')), may hold values from -6 to 6
- w_embed: bfloat16 [2048, 512], replicated, may hold values from -0.125 to 0.125
- w_query: bfloat16 [512, 512], replicated, may hold values from -0.25 to 0.25
- w_key: bfloat16 [512, 512], replicated, may hold values from -0.25 to 0.25
- w_value: bfloat16 [512, 512], replicated, may hold values from -0.25 to 0.25
- w_out: bfloat16 [512, 512], replicated, may hold values from -0.25 to 0.25
- proj: bfloat16 [256, 131072], P(None, ('var', 'grp')), may hold values from -0.0625 to 0.0625
- cotangent: bfloat16 [131072, 512], P(('var', 'grp')), may hold values from -6 to 6
Outputs:
- output: bfloat16 [131072, 512], P(('var', 'grp'))
- grad_embed: float32 [2048, 512], replicated
- grad_attn: float32 [4, 512, 512], replicated
All inputs are finite; a program needn't handle non-finite values.
Results may differ from a plain program's by a relative error of at most 0.019.
Values sent between devices are 32-bit elements; how exact they have to be, the bound alone decides.
A program may use at most 128 MiB of HBM per device.

v0:
```python
import math

import jax
import jax.numpy as jnp
from jax import lax
from jax.sharding import PartitionSpec as P

HEADS = 8


def head_norm(values):
    shaped = values.reshape(values.shape[0], HEADS, -1)
    factor = lax.rsqrt(jnp.mean(shaped * shaped, axis=-1, keepdims=True) + 1e-06)
    return (shaped * factor, factor)


def norm_back(grad_n, normed, factor):
    return factor * (grad_n - normed * jnp.mean(grad_n * normed, axis=-1, keepdims=True))


def contract_rows(left, right, precision=None):
    return lax.dot_general(
        left,
        right,
        (((0,), (0,)), ((), ())),
        preferred_element_type=jnp.float32,
        precision=precision,
    )


def split_parts(values, axis):
    upper = values.astype(jnp.bfloat16)
    rest = values - upper.astype(jnp.float32)
    middle = rest.astype(jnp.bfloat16)
    lower = (rest - middle.astype(jnp.float32)).astype(jnp.bfloat16)
    return jnp.concatenate([upper, middle, lower], axis)


def fold_parts(values, axis):
    first, second, third = jnp.split(values, 3, axis)
    return first + second + third


def weight_totals(embed_part, attn_part):
    return lax.psum((embed_part, attn_part), ("var", "grp"))


def local(series, w_embed, w_query, w_key, w_value, w_out, proj, cotangent):
    rows = series.shape[0]
    proj_rows = proj.shape[0]
    width = w_query.shape[0]
    scale = 1.0 / math.sqrt(width // HEADS)
    total_rows = rows * lax.axis_size("var") * lax.axis_size("grp")
    hid = jnp.dot(series, w_embed, preferred_element_type=jnp.float32).astype(jnp.bfloat16)
    kv_weights = jnp.concatenate([w_key, w_value], 1)
    kv_back = jnp.concatenate([w_key.T, w_value.T], 0)
    kv_rows = jnp.dot(hid, kv_weights, preferred_element_type=jnp.float32)
    kv_part = fold_parts(
        jnp.dot(proj, split_parts(kv_rows, 1), preferred_element_type=jnp.float32), 1
    )
    keyproj, valproj = lax.psum((kv_part[:, :width], kv_part[:, width:]), ("var", "grp"))
    key_n, key_r = head_norm(keyproj)
    key_nb = key_n.astype(jnp.bfloat16)
    val_parts = split_parts(valproj, 0).reshape(3 * proj_rows, HEADS, -1)
    val_h = val_parts[:proj_rows]
    query = jnp.dot(hid, w_query, preferred_element_type=jnp.float32)
    query_n, query_r = head_norm(query)
    query_nb = query_n.astype(jnp.bfloat16)
    scores = (
        jnp.einsum("nhd,khd->nhk", query_nb, key_nb, preferred_element_type=jnp.float32) * scale
    )
    expo = jnp.exp(scores)
    probs = expo / jnp.sum(expo, axis=-1, keepdims=True)
    probs_b = probs.astype(jnp.bfloat16)
    attended = jnp.einsum("nhk,khd->nhd", probs_b, val_h, preferred_element_type=jnp.float32)
    attended = attended.astype(jnp.bfloat16).reshape(rows, width)
    output = (
        hid.astype(jnp.float32) + jnp.dot(attended, w_out, preferred_element_type=jnp.float32)
    ).astype(jnp.bfloat16)
    grad_att = (
        jnp.dot(cotangent, w_out.T, preferred_element_type=jnp.float32)
        .astype(jnp.bfloat16)
        .reshape(rows, HEADS, -1)
    )
    gw_out = contract_rows(attended, cotangent)
    grad_probs = fold_parts(
        jnp.einsum("nhd,khd->nhk", grad_att, val_parts, preferred_element_type=jnp.float32), 2
    )
    grad_val = jnp.einsum(
        "nhk,nhd->khd", probs_b, grad_att, preferred_element_type=jnp.float32
    ).reshape(proj_rows, width)
    grad_scores = (
        probs * (grad_probs - jnp.sum(probs * grad_probs, axis=-1, keepdims=True)) * scale
    ).astype(jnp.bfloat16)
    grad_qn = jnp.einsum("nhk,khd->nhd", grad_scores, key_nb, preferred_element_type=jnp.float32)
    grad_kn = jnp.einsum(
        "nhk,nhd->khd", grad_scores, query_nb, preferred_element_type=jnp.float32
    ).reshape(proj_rows, width)
    grad_query = norm_back(grad_qn, query_n, query_r).reshape(rows, width).astype(jnp.bfloat16)
    gw_query = contract_rows(hid, grad_query)
    grad_kn, grad_val = lax.psum((grad_kn, grad_val), ("var", "grp"))
    grad_key = norm_back(grad_kn.reshape(proj_rows, HEADS, -1), key_n, key_r).reshape(
        proj_rows, width
    )
    grad_both = jnp.concatenate([grad_key, grad_val], 1)
    grad_kv = fold_parts(contract_rows(proj, split_parts(grad_both, 1)), 1)
    gw_kv = fold_parts(contract_rows(hid, split_parts(grad_kv, 1)), 1)
    gw_key_part = gw_kv[:, :width]
    gw_value_part = gw_kv[:, width:]
    from_kv = fold_parts(
        jnp.dot(split_parts(grad_kv, 0), kv_back, preferred_element_type=jnp.float32), 0
    )
    grad_hid = (
        cotangent.astype(jnp.float32)
        + jnp.dot(grad_query, w_query.T, preferred_element_type=jnp.float32)
        + from_kv
    ).astype(jnp.bfloat16)
    gw_embed = contract_rows(series, grad_hid)
    norm = 1.0 / math.sqrt(total_rows)
    embed_sum, attn_sum = weight_totals(
        gw_embed, jnp.stack([gw_query, gw_key_part, gw_value_part, gw_out])
    )
    grad_attn = attn_sum * norm
    return (output, embed_sum * norm, grad_attn)


def solution(mesh):
    return jax.shard_map(
        local,
        mesh=mesh,
        in_specs=(
            P(("var", "grp"), None),
            P(),
            P(),
            P(),
            P(),
            P(),
            P(None, ("var", "grp")),
            P(("var", "grp"), None),
        ),
        out_specs=(P(("var", "grp"), None), P(), P()),
        check_vma=False,
    )
```

profile of v0, /device:TPU:1, one launch (start us, length us, event | category | flops | bytes accessed | tf_op | source)
XLA Modules:
  0.0 609.1 jit_solution(14358813383048530701)
XLA Ops:
  7.2 0.0 copy-start
  7.2 0.0 all-reduce.11.cloned.1.call-start
  7.2 1.5 copy-done
  8.8 4.6 convolution_convert_fusion.1
  13.4 0.0 copy-start.8
  13.4 0.0 copy-start.14
  13.4 1.4 fusion.73
  14.9 1.9 fusion.22
  16.8 0.2 slice_add_fusion.8
  17.0 1.0 fusion.74
  18.0 0.0 all-reduce.11.cloned.1.call-update
  18.0 0.2 all-reduce.9.cloned.1.call-start
  18.3 1.8 multiply_reduce_fusion.1
  20.1 3.1 convolution_convert_fusion
  23.2 145.8 %all-reduce.11.cloned.1.call-done = (f32[256,512]{0,1:T(8,128)}, f32[256,512]{0,1:T(8,128)}) async-done(((f32[256,512]{0,1:T(8,128)}, f32[256,512]{0,1:T(8,128)}), (f32[256,512]{0,1:T(8,128)}, f32[256,512]{0,1:T(8,128)})) %all-reduce.11.cloned.1.call-update) | async-done | bytes 1048592 | tf_op jit(solution)/shard_map/psum | solution.py:61
  169.0 1.2 multiply_reduce_fusion.3
  170.2 1.3 fusion.61
  171.5 0.1 pad_maximum_fusion.2
  171.6 10.1 %convolution_bitcast_fusion = f32[1024,8,768]{0,2,1:T(8,128)} fusion(bf16[768,8,64]{0,2,1:T(8,128)(2,1)S(1)} %bitcast.124, bf16[1024,8,64]{0,2,1:T(8,128)(2,1)S(1)} %bitcast.125), kind=kOutput, calls=%fused_computation.1 | convolution fusion | flops 805306368 | bytes 27000832 | tf_op jit(solution)/shard_map/nhd,khd->nhk/dot_general | solution.py:87
  181.7 1.6 bitcast_reduce_fusion
  183.3 3.2 copy-done.3
  186.5 2.4 fusion.38
  188.9 23.2 %fusion.26 = f32[8,64,256]{2,1,0:T(8,128)} fusion(f32[1024,512]{0,1:T(8,128)S(1)} %get-tuple-element.29, f32[1024,8]{0,1:T(8,128)S(1)} %add_rsqrt_fusion, f32[8,256,1024]{2,1,0:T(8,128)} %copy-done.3, f32[1024,8]{0,1:T(8,128)S(1)} %get-tuple-element.30, f32[1024,8,768]{0,2,1:T(8,128)} %convolution_bitcast_fusion), kind=kOutput, calls=%fused_computation.37 | convolution fusion | flops 296755456 | bytes 69828608 | tf_op jit(solution)/shard_map/nhk,nhd->khd/dot_general | solution.py:96
  212.0 25.8 %fusion.35 = (f32[1024,8]{0,1:T(8,128)S(1)}, f32[8,64,1024]{2,1,0:T(8,128)}) fusion(f32[1024,512]{0,1:T(8,128)S(1)} %get-tuple-element.29, f32[1024,8]{0,1:T(8,128)S(1)} %add_rsqrt_fusion, f32[1024,8]{0,1:T(8,128)S(1)} %get-tuple-element.30, f32[8,256,1024]{2,1,0:T(8,128)} %copy-done.3, f32[256,512]{0,1:T(8,128)S(1)} %copy-done.2, ...), kind=kOutput, calls=%fused_computation.50 | convolution fusion | flops 297533696 | bytes 71966720 | tf_op jit(solution)/shard_map/nhk,khd->nhd/dot_general | solution.py:95
  237.9 6.0 fusion.47
  243.9 0.0 all-reduce.9.cloned.1.call-update
  243.9 0.3 all-reduce.7.cloned.1.call-start
  244.2 0.0 copy-start.16
  244.2 0.0 copy-start.9
  244.2 2.3 fusion.37
  246.6 1.7 convolution_bitcast_fusion.3
  248.3 1.8 convolution_bitcast_fusion.4
  250.1 140.2 %all-reduce.9.cloned.1.call-done = (f32[256,512]{0,1:T(8,128)}, f32[256,512]{0,1:T(8,128)}) async-done(((f32[256,512]{0,1:T(8,128)}, f32[256,512]{0,1:T(8,128)}), (f32[256,512]{0,1:T(8,128)}, f32[256,512]{0,1:T(8,128)})) %all-reduce.9.cloned.1.call-update) | async-done | bytes 1048592 | tf_op jit(solution)/shard_map/psum | solution.py:101
  390.3 1.2 multiply_reduce_fusion.2
  391.5 1.1 bitcast_multiply_fusion.1
  392.6 1.1 fusion.57
  393.7 0.1 fusion.58
  393.8 1.8 convolution_bitcast_fusion.1
  395.7 2.0 fusion.72
  397.7 0.0 copy-start.5
  397.7 0.0 copy-start.10
  397.7 0.9 fusion.32
  398.6 0.5 copy-done.5
  399.0 0.6 copy-done.10
  399.7 3.5 fusion.14
  403.2 0.0 copy-start.20
  403.2 0.7 slice_add_fusion.4
  403.9 0.8 copy-done.6
  404.7 0.1 copy-done.18
  404.8 0.2 copy-done.20
  405.0 7.5 %fusion.8 = f32[3072,512]{1,0:T(8,128)} fusion(bf16[1024,1024]{0,1:T(8,128)(2,1)S(1)} %get-tuple-element.15, bf16[1024,1024]{0,1:T(8,128)(2,1)S(1)} %get-tuple-element.14, bf16[1024,1024]{0,1:T(8,128)(2,1)S(1)} %copy-done.6, bf16[512,512]{0,1:T(8,128)(2,1)S(1)} %bitcast.132, bf16[512,512]{0,1:T(8,128)(2,1)S(1)} %bitcast.133), kind=kOutput, calls=%fused_computation.17 | convolution fusion | flops 3242196992 | bytes 13631488 | tf_op jit(solution)/shard_map/dot_general | solution.py:111
  412.5 10.2 %convolution_bitcast_fusion.2 = f32[2048,512]{0,1:T(8,128)} fusion(bf16[1024,2048]{1,0:T(8,128)(2,1)} %param.8, f32[3072,512]{1,0:T(8,128)} %fusion.8, bf16[1024,512]{1,0:T(8,128)(2,1)} %param.15, bf16[1024,512]{0,1:T(8,128)(2,1)} %bitcast.129, bf16[512,512]{1,0:T(8,128)(2,1)} %param.10), kind=kOutput, calls=%fused_computation.39 | convolution fusion | flops 2687500288 | bytes 17301504 | tf_op jit(solution)/shard_map/dot_general | solution.py:22
  422.7 0.2 slice_bitcast_fusion.1
  422.9 1.0 copy-done.12
  423.9 0.3 copy-done.13
  424.2 2.5 pad_maximum_fusion
  426.7 0.0 all-reduce.7.cloned.1.call-update
  426.7 1.0 copy-done.21
  427.7 0.3 copy-done.23
  428.1 1.7 add_convert_fusion
  429.8 157.6 %all-reduce.7.cloned.1.call-done = (f32[2048,512]{0,1:T(8,128)}, f32[4,512,512]{2,1,0:T(8,128)}) async-done(((f32[2048,512]{0,1:T(8,128)}, f32[4,512,512]{2,1,0:T(8,128)}), (f32[2048,512]{0,1:T(8,128)}, f32[4,512,512]{2,1,0:T(8,128)})) %all-reduce.7.cloned.1.call-update) | async-done | bytes 8388624 | tf_op jit(solution)/shard_map/psum | solution.py:45
  587.4 5.0 broadcast_multiply_fusion.1
  592.3 5.3 copy.15
  597.7 4.9 broadcast_multiply_fusion
  (33 shorter events, 0.1 us)
Async XLA Ops:
  7.2 1.6 copy-start
  7.2 161.8 %all-reduce.11.cloned.1.call-start = ((), (), s32[]{:S(2)}) async-start(), calls=%async_computation.2 | async-start | bytes 2097152 | tf_op jit(solution)/shard_map/psum | solution.py:61
  8.8 4.6 copy-start.17
  8.8 4.6 copy-start.19
  13.4 4.9 copy-start.8
  13.4 1.4 copy-start.14
  18.0 372.2 %all-reduce.9.cloned.1.call-start = ((), (), s32[]{:S(2)}) async-start(), calls=%async_computation.1 | async-start | bytes 2097152 | tf_op jit(solution)/shard_map/psum | solution.py:101
  169.0 2.6 copy-start.4
  171.6 10.1 %copy-start.2 = (f32[256,512]{0,1:T(8,128)S(1)}, f32[256,512]{0,1:T(8,128)}, u32[]{:S(2)}) copy-start(f32[256,512]{0,1:T(8,128)} %get-tuple-element.11) | copy-start | bytes 1572868
  183.3 3.2 copy-start.3
  243.9 343.4 %all-reduce.7.cloned.1.call-start = ((), (), s32[]{:S(2)}) async-start(), calls=%async_computation | async-start | bytes 16777216 | tf_op jit(solution)/shard_map/psum | solution.py:45
  244.2 2.4 copy-start.16
  244.2 2.4 copy-start.22
  244.2 4.0 copy-start.9
  246.6 1.7 copy-start.11
  248.3 145.6 %copy-start.15 = (bf16[256,1024]{1,0:T(8,128)(2,1)S(1)}, bf16[256,1024]{1,0:T(8,128)(2,1)}, u32[]{:S(2)}) copy-start(bf16[256,1024]{1,0:T(8,128)(2,1)} %param.14) | copy-start | bytes 1572868
  390.3 3.4 copy-start.7
  397.7 1.4 copy-start.5
  397.7 2.0 copy-start.10
  403.1 1.6 copy-start.6
  403.2 1.7 copy-start.18
  403.2 1.8 copy-start.20
  422.7 1.2 copy-start.12
  422.7 1.5 copy-start.13
  426.7 1.0 copy-start.21
  426.7 1.4 copy-start.23
  597.7 4.9 copy-start.1
Sparse Core Ops, SparseCore 0:
  18.1 150.8 all-reduce.10
  244.1 146.1 all-reduce.8
  426.8 160.4 all-reduce.6
where the time goes:
time: 610 us; the launch traced here: 609 us
  waiting for transfers between devices  444 us (73%)
  matrix products  110 us (18%)
  other arithmetic  24.5 us (4%)
  local copies, waits for them, and re-layouts  16.3 us (3%)
  between operations  14.1 us (2%)
    psum x1, waiting for transfers between devices, weight_totals(): return lax.psum((embed_part, attn_part), ('var', 'grp'))  158 us
    psum x1, waiting for transfers between devices, local(): lax.psum((kv_part[:, :width], kv_part[:, width:]), ('var', 'grp'))  146 us
    psum x1, waiting for transfers between devices, local(): grad_kn, grad_val = lax.psum((grad_kn, grad_val), ('var', 'grp'))  140 us
    dot_general x1, matrix products, local(): jnp.einsum('nhk,khd->nhd', grad_scores, key_nb, preferred_element_type=jn...  25.8 us
    dot_general x1, matrix products, local(): jnp.einsum('nhk,nhd->khd', grad_scores, query_nb, preferred_element_type=...  23.2 us
    dot_general x5, matrix products, contract_rows(): lax.dot_general(left, right, (((0,), (0,)), ((), ())), preferred_element_...  19 us
    unnamed x49, local copies, waits for them, and re-layouts  15.1 us
  transfers between devices with their start and end apart: 3, of which 3 were waited for; matrix products, arithmetic and copies ran while one was open for 2% of the time, Pallas kernels for 0%

commit v1 on v0

v1 whole, which is shorter than its diff:
```python
import functools
import math

import jax
import jax.numpy as jnp
from jax import lax
from jax.experimental import pallas as pl
from jax.experimental.pallas import tpu as pltpu
from jax.sharding import PartitionSpec as P

HEADS = 8
MESH = pl.DeviceIdType.MESH
F32 = jnp.float32
BF16 = jnp.bfloat16
VMEM = pltpu.VMEM


def head_norm(values):
    shaped = values.reshape(values.shape[0], HEADS, -1)
    factor = lax.rsqrt(jnp.mean(shaped * shaped, axis=-1, keepdims=True) + 1e-06)
    return (shaped * factor, factor)


def norm_back(grad_n, normed, factor):
    return factor * (grad_n - normed * jnp.mean(grad_n * normed, axis=-1, keepdims=True))


def contract_rows(left, right, precision=None):
    return lax.dot_general(
        left,
        right,
        (((0,), (0,)), ((), ())),
        preferred_element_type=F32,
        precision=precision,
    )


def split_parts(values, axis):
    upper = values.astype(BF16)
    rest = values - upper.astype(F32)
    middle = rest.astype(BF16)
    lower = (rest - middle.astype(F32)).astype(BF16)
    return jnp.concatenate([upper, middle, lower], axis)


def fold_parts(values, axis):
    first, second, third = jnp.split(values, 3, axis)
    return first + second + third


def position():
    var = lax.axis_index("var")
    return {
        "x": lax.div(var, 8),
        "y": lax.rem(lax.div(var, 2), 4),
        "c": lax.rem(var, 2),
        "z": lax.axis_index("grp"),
    }


def moved(place, **steps):
    there = dict(place)
    for axis, step in steps.items():
        there[axis] = lax.rem(place[axis] + step, 2 if axis == "c" else 4)
    return (there["x"] * 8 + there["y"] * 2 + there["c"], there["z"])


def greet(devices):
    barrier = pltpu.get_barrier_semaphore()
    for device in devices:
        pl.semaphore_signal(barrier, inc=1, device_id=device, device_id_type=MESH)
    return lambda: pl.semaphore_wait(barrier, len(devices))


def sum_small_kernel(in_ref, out_ref, half, from_core, from_plane, from_x, send, recv):
    here = position()
    core, plane = here["c"], here["y"] * 4 + here["z"]
    base = core * 512

    def plane_device(step):
        there = lax.rem(plane + step, 16)
        return (here["x"] * 8 + lax.div(there, 4) * 2 + core, lax.rem(there, 4))

    others = [moved(here, c=1)]
    others += [moved(here, x=step) for step in (1, 2, 3)]
    others += [plane_device(step) for step in range(1, 16)]
    greet(others)()
    count = [0]

    def copy(src, dst, device):
        slot = count[0]
        count[0] += 1
        made = pltpu.make_async_remote_copy(
            src_ref=src,
            dst_ref=dst,
            send_sem=send.at[slot],
            recv_sem=recv.at[slot],
            device_id=device,
            device_id_type=MESH,
        )
        made.start()
        return made

    across = copy(in_ref.at[pl.ds((1 - core) * 512, 512)], from_core, moved(here, c=1))
    across.wait()
    half[...] = in_ref[pl.ds(pl.multiple_of(base, 512), 512)] + from_core[...]
    sent = []
    for step in range(1, 16):
        there = lax.rem(plane + step, 16)
        sent.append(
            copy(half.at[pl.ds(there * 32, 32)], from_plane.at[step], plane_device(step))
        )
    own = pl.multiple_of(plane * 32, 32)
    total = half[pl.ds(own, 32)]
    for made in sent:
        made.wait_recv()
    for step in range(1, 16):
        total = total + from_plane[step]
    from_x[here["x"]] = total
    shares = [
        copy(from_x.at[here["x"]], from_x.at[here["x"]], moved(here, x=step))
        for step in (1, 2, 3)
    ]
    for made in shares:
        made.wait_recv()
    whole = (from_x[0] + from_x[1]) + (from_x[2] + from_x[3])
    mine = out_ref.at[pl.ds(base + own, 32)]
    mine[...] = whole
    spread = [copy(mine, mine, plane_device(step)) for step in range(1, 16)]
    passed = [copy(mine, mine, moved(here, c=1))]
    for step in range(1, 16):
        spread[step - 1].wait_recv()
        origin = lax.rem(plane + 16 - step, 16)
        piece = out_ref.at[pl.ds(base + origin * 32, 32)]
        passed.append(copy(piece, piece, moved(here, c=1)))
    for made in passed:
        made.wait_recv()
    for made in sent + shares + spread + passed:
        made.wait_send()


def sum_small(values):
    copies = 1 + 15 + 3 + 15 + 16
    return pl.pallas_call(
        sum_small_kernel,
        out_shape=jax.ShapeDtypeStruct((1024, 128), F32),
        in_specs=[pl.BlockSpec(memory_space=VMEM)],
        out_specs=pl.BlockSpec(memory_space=VMEM),
        scratch_shapes=[
            VMEM((512, 128), F32),
            VMEM((512, 128), F32),
            VMEM((16, 32, 128), F32),
            VMEM((4, 32, 128), F32),
            pltpu.SemaphoreType.DMA((copies,)),
            pltpu.SemaphoreType.DMA((copies,)),
        ],
        compiler_params=pltpu.CompilerParams(collective_id=0, has_side_effects=True),
    )(values)


ORDERS = (("x", "y", "z"), ("y", "z", "x"), ("z", "x", "y"))
UNITS = 6


def sum_large_kernel(in_ref, out_ref, work, from_core, ring1, ring2, last, send, recv):
    here = position()
    core = here["c"]
    base = core * 512
    ready = greet(
        [moved(here, c=1)]
        + [moved(here, **{axis: step}) for axis in "xyz" for step in (1, 2, 3)]
    )
    ready()
    count = [0]
    sent = []

    def copy(src, dst, device):
        slot = count[0]
        count[0] += 1
        made = pltpu.make_async_remote_copy(
            src_ref=src,
            dst_ref=dst,
            send_sem=send.at[slot],
            recv_sem=recv.at[slot],
            device_id=device,
            device_id_type=MESH,
        )
        made.start()
        sent.append(made)
        return made

    groups = range(3)
    units = [pl.ds(group * UNITS, UNITS) for group in groups]

    def rows(start, size, step):
        return pl.ds(pl.multiple_of(start, step), size)

    across = [
        copy(
            in_ref.at[units[group], rows((1 - core) * 512, 512, 512)],
            from_core.at[group],
            moved(here, c=1),
        )
        for group in groups
    ]
    for group in groups:
        across[group].wait_recv()

        @pl.loop(0, UNITS)
        def _(unit):
            work[group, unit] = (
                in_ref[group * UNITS + unit, rows(base, 512, 512)] + from_core[group, unit]
            )

    offset = [0, 0, 0]
    for level, size, ring in ((0, 128, ring1), (1, 32, ring2)):
        half = size // 2

        def part(group, step, which):
            axis = ORDERS[group][level]
            chunk = lax.rem(here[axis] + step, 4)
            return (group, slice(None), rows(offset[group] + chunk * size + which * half, half, half))

        state = []
        for group in groups:
            axis = ORDERS[group][level]
            up, down = moved(here, **{axis: 1}), moved(here, **{axis: 3})
            state.append(
                (
                    copy(work.at[part(group, 2, 0)], ring.at[group, 0], up),
                    copy(work.at[part(group, 2, 1)], ring.at[group, 1], down),
                    copy(work.at[part(group, 1, 1)], ring.at[group, 2], up),
                    copy(work.at[part(group, 3, 0)], ring.at[group, 3], down),
                    up,
                    down,
                )
            )
        more = []
        for group in groups:
            relay_a, relay_b, _, _, up, down = state[group]
            relay_a.wait_recv()
            where = part(group, 1, 0)
            work[where] = work[where] + ring[group, 0]
            more_a = copy(work.at[where], ring.at[group, 4], up)
            relay_b.wait_recv()
            where = part(group, 3, 1)
            work[where] = work[where] + ring[group, 1]
            more.append((more_a, copy(work.at[where], ring.at[group, 5], down)))
        for group in groups:
            _, _, direct_b, direct_a, _, _ = state[group]
            more_a, more_b = more[group]
            direct_a.wait_recv()
            more_a.wait_recv()
            where = part(group, 0, 0)
            work[where] = work[where] + ring[group, 3] + ring[group, 4]
            direct_b.wait_recv()
            more_b.wait_recv()
            where = part(group, 0, 1)
            work[where] = work[where] + ring[group, 2] + ring[group, 5]
        for group in groups:
            offset[group] = offset[group] + here[ORDERS[group][level]] * size

    direct = []
    for group in groups:
        axis = ORDERS[group][2]
        direct.append(
            [
                copy(
                    work.at[
                        group,
                        :,
                        rows(offset[group] + lax.rem(here[axis] + step, 4) * 8, 8, 8),
                    ],
                    last.at[group, step - 1],
                    moved(here, **{axis: step}),
                )
                for step in (1, 2, 3)
            ]
        )
    spread = []
    for group in groups:
        axis = ORDERS[group][2]
        for made in direct[group]:
            made.wait_recv()
        own = offset[group] + here[axis] * 8
        mine = (units[group], rows(base + own, 8, 8))
        out_ref[mine] = (
            work[group, :, rows(own, 8, 8)] + last[group, 0] + last[group, 1] + last[group, 2]
        )
        spread.append(
            [
                copy(out_ref.at[mine], out_ref.at[mine], moved(here, **{axis: step}))
                for step in (1, 2, 3)
            ]
        )
    for group in groups:
        for made in spread[group]:
            made.wait_recv()

    arrivals = []
    for level, size in ((1, 32), (0, 128)):
        half = size // 2
        state = []

        def piece(group, step, start=0, length=None):
            axis = ORDERS[group][level]
            chunk = lax.rem(here[axis] + step, 4)
            length = size if length is None else length
            return out_ref.at[
                units[group], rows(base + offset[group] + chunk * size + start, length, half)
            ]

        for group in groups:
            axis = ORDERS[group][level]
            offset[group] = offset[group] - here[axis] * size
            up, down = moved(here, **{axis: 1}), moved(here, **{axis: 3})
            own = piece(group, 0)
            state.append((copy(own, own, up), copy(own, own, down), up, down))
            if level == 0:
                arrivals.append(copy(own, own, moved(here, c=1)))
        forwards = []
        for group in groups:
            from_down, from_up, up, down = state[group]
            from_down.wait_recv()
            got = piece(group, 3, 0, half)
            forward_a = copy(got, got, up)
            from_up.wait_recv()
            got = piece(group, 1, half, half)
            forwards.append((forward_a, copy(got, got, down)))
            if level == 0:
                for step in (1, 3):
                    got = piece(group, step)
                    arrivals.append(copy(got, got, moved(here, c=1)))
        for group in groups:
            for made in forwards[group]:
                made.wait_recv()
            if level == 0:
                got = piece(group, 2)
                arrivals.append(copy(got, got, moved(here, c=1)))
    for made in arrivals:
        made.wait_recv()
    for made in sent:
        made.wait_send()


def sum_large(values):
    copies = 3 * (1 + 6 + 6 + 3 + 3 + 4 + 4 + 4)
    return pl.pallas_call(
        sum_large_kernel,
        out_shape=jax.ShapeDtypeStruct((18, 1024, 128), F32),
        in_specs=[pl.BlockSpec(memory_space=VMEM)],
        out_specs=pl.BlockSpec(memory_space=VMEM),
        scratch_shapes=[
            VMEM((3, UNITS, 512, 128), F32),
            VMEM((3, UNITS, 512, 128), F32),
            VMEM((3, 6, UNITS, 64, 128), F32),
            VMEM((3, 6, UNITS, 16, 128), F32),
            VMEM((3, 3, UNITS, 8, 128), F32),
            pltpu.SemaphoreType.DMA((copies,)),
            pltpu.SemaphoreType.DMA((copies,)),
        ],
        compiler_params=pltpu.CompilerParams(
            collective_id=1, has_side_effects=True, vmem_limit_bytes=56 * 1024 * 1024
        ),
    )(values)


def to_units(values):
    rows, columns = values.shape
    lanes = values.reshape(rows, columns // 128, 128).transpose(1, 0, 2)
    return lanes.reshape(-1, 1024, 128)


def from_units(units, rows, columns):
    lanes = units.reshape(columns // 128, rows, 128)
    return lanes.transpose(1, 0, 2).reshape(rows, columns)


def local(series, w_embed, w_query, w_key, w_value, w_out, proj, cotangent):
    rows = series.shape[0]
    proj_rows = proj.shape[0]
    width = w_query.shape[0]
    scale = 1.0 / math.sqrt(width // HEADS)
    total_rows = rows * lax.axis_size("var") * lax.axis_size("grp")
    hid = jnp.dot(series, w_embed, preferred_element_type=F32).astype(BF16)
    kv_weights = jnp.concatenate([w_key, w_value], 1)
    kv_back = jnp.concatenate([w_key.T, w_value.T], 0)
    ph_part = jnp.dot(proj, hid, preferred_element_type=F32)
    ph = from_units(sum_small(to_units(ph_part)[0])[None], proj_rows, width)
    kv = fold_parts(jnp.dot(split_parts(ph, 0), kv_weights, preferred_element_type=F32), 0)
    keyproj, valproj = kv[:, :width], kv[:, width:]
    key_n, key_r = head_norm(keyproj)
    key_nb = key_n.astype(BF16)
    val_parts = split_parts(valproj, 0).reshape(3 * proj_rows, HEADS, -1)
    val_h = val_parts[:proj_rows]
    query = jnp.dot(hid, w_query, preferred_element_type=F32)
    query_n, query_r = head_norm(query)
    query_nb = query_n.astype(BF16)
    scores = (
        jnp.einsum("nhd,khd->nhk", query_nb, key_nb, preferred_element_type=F32) * scale
    )
    expo = jnp.exp(scores)
    probs = expo / jnp.sum(expo, axis=-1, keepdims=True)
    probs_b = probs.astype(BF16)
    attended = jnp.einsum("nhk,khd->nhd", probs_b, val_h, preferred_element_type=F32)
    attended = attended.astype(BF16).reshape(rows, width)
    output = (
        hid.astype(F32) + jnp.dot(attended, w_out, preferred_element_type=F32)
    ).astype(BF16)
    grad_att = (
        jnp.dot(cotangent, w_out.T, preferred_element_type=F32)
        .astype(BF16)
        .reshape(rows, HEADS, -1)
    )
    gw_out = contract_rows(attended, cotangent)
    grad_probs = fold_parts(
        jnp.einsum("nhd,khd->nhk", grad_att, val_parts, preferred_element_type=F32), 2
    )
    grad_val = jnp.einsum(
        "nhk,nhd->khd", probs_b, grad_att, preferred_element_type=F32
    ).reshape(proj_rows, width)
    grad_scores = (
        probs * (grad_probs - jnp.sum(probs * grad_probs, axis=-1, keepdims=True)) * scale
    ).astype(BF16)
    grad_qn = jnp.einsum("nhk,khd->nhd", grad_scores, key_nb, preferred_element_type=F32)
    grad_kn = jnp.einsum(
        "nhk,nhd->khd", grad_scores, query_nb, preferred_element_type=F32
    ).reshape(proj_rows, width)
    grad_query = norm_back(grad_qn, query_n, query_r).reshape(rows, width).astype(BF16)
    gw_query = contract_rows(hid, grad_query)
    grad_hid = (
        cotangent.astype(F32) + jnp.dot(grad_query, w_query.T, preferred_element_type=F32)
    ).astype(BF16)
    gw_embed = contract_rows(series, grad_hid)
    proj_series = jnp.dot(proj, series, preferred_element_type=F32)
    totals = sum_large(
        jnp.concatenate(
            [
                to_units(part)
                for part in (gw_embed, proj_series, gw_query, gw_out, grad_kn, grad_val)
            ],
            0,
        )
    )
    gw_embed = from_units(totals[0:8], 2048, width)
    proj_series = from_units(totals[8:12], proj_rows, 2048)
    gw_query = from_units(totals[12:14], width, width)
    gw_out = from_units(totals[14:16], width, width)
    grad_kn = from_units(totals[16:17], proj_rows, width)
    grad_val = from_units(totals[17:18], proj_rows, width)
    grad_key = norm_back(grad_kn.reshape(proj_rows, HEADS, -1), key_n, key_r).reshape(
        proj_rows, width
    )
    grad_both = jnp.concatenate([grad_key, grad_val], 1)
    back = fold_parts(
        jnp.dot(split_parts(grad_both, 0), kv_back, preferred_element_type=F32), 0
    )
    high = lax.Precision.HIGHEST
    gw_embed = gw_embed + contract_rows(proj_series, back, high)
    gw_key = contract_rows(ph, grad_key, high)
    gw_value = contract_rows(ph, grad_val, high)
    norm = 1.0 / math.sqrt(total_rows)
    grad_attn = jnp.stack([gw_query, gw_key, gw_value, gw_out]) * norm
    return (output, gw_embed * norm, grad_attn)


def solution(mesh):
    return jax.shard_map(
        local,
        mesh=mesh,
        in_specs=(
            P(("var", "grp"), None),
            P(),
            P(),
            P(),
            P(),
            P(),
            P(None, ("var", "grp")),
            P(("var", "grp"), None),
        ),
        out_specs=(P(("var", "grp"), None), P(), P()),
        check_vma=False,
    )
```

time: 610 us -> 276 us (0.45)
  waiting for transfers between devices: 444 us -> 0 us
  Pallas kernels: 0 us -> 106 us
  local copies, waits for them, and re-layouts: 16.3 us -> 50.3 us
  other arithmetic: 24.5 us -> 10.9 us
  between operations: 14.1 us -> 1.13 us
    psum x3 -> x0, waiting for transfers between devices: 444 us -> none  [the longest x1 158 us: weight_totals(): return lax.psum((embed_part, attn_part), ('var', 'grp'))]
    pallas_call x0 -> x2, Pallas kernels: none -> 106 us  [the longest x1 75.9 us: sum_large(): pl.pallas_call(sum_large_kernel, out_shape=jax.ShapeDtypeStruct((18, 1024...]
    reshape x0 -> x5, local copies, waits for them, and re-layouts: none -> 9.68 us  [the longest x3 7.83 us: to_units(): lanes = values.reshape(rows, columns // 128, 128).transpose(1, 0, 2)]
    slice x1 -> x7, local copies, waits for them, and re-layouts: 1.04 us -> 8.24 us  [the longest x1 2.67 us: local(): gw_query = from_units(totals[12:14], width, width)]
    another operation x1 -> x5, local copies, waits for them, and re-layouts: 0.2 us -> 7.06 us  [the longest x2 3.04 us: to_units(): lanes = values.reshape(rows, columns // 128, 128).transpose(1, 0, 2)]
    dot_general x12 -> x13, matrix products: 67.9 us -> 61.4 us  [the longest x1 25.8 us: local(): jnp.einsum('nhk,khd->nhd', grad_scores, key_nb, preferred_element_type=F32)]
    dot_general x5 -> x6, matrix products: 19 us -> 21.6 us  [contract_rows(): lax.dot_general(left, right, (((0,), (0,)), ((), ())), preferred_element_...]
    unnamed x49 -> x81, local copies, waits for them, and re-layouts: 15.1 us -> 14.8 us
  transfers between devices with their start and end apart: 3 -> 0, of which waited for: 3 -> 0; matrix products, arithmetic and copies ran while one was open for 2% -> 0% of each run, Pallas kernels for 0% -> 0%
where the time goes in v1:
time: 276 us; the launch traced here: 275 us
  matrix products  106 us (38%)
  Pallas kernels  106 us (38%)
  local copies, waits for them, and re-layouts  50.3 us (18%)
  other arithmetic  10.9 us (4%)
    pallas_call x1, Pallas kernels, sum_large(): pl.pallas_call(sum_large_kernel, out_shape=jax.ShapeDtypeStruct((18, 1024...  75.9 us
    pallas_call x1, Pallas kernels, sum_small(): pl.pallas_call(sum_small_kernel, out_shape=jax.ShapeDtypeStruct((1024, 12...  30.4 us
    dot_general x1, matrix products, local(): jnp.einsum('nhk,khd->nhd', grad_scores, key_nb, preferred_element_type=F32)  25.8 us
    dot_general x1, matrix products, local(): jnp.einsum('nhk,nhd->khd', grad_scores, query_nb, preferred_element_type=...  23.1 us
    dot_general x6, matrix products, contract_rows(): lax.dot_general(left, right, (((0,), (0,)), ((), ())), preferred_element_...  21.6 us
    unnamed x81, local copies, waits for them, and re-layouts  14.8 us
    dot_general x1, matrix products, local(): jnp.einsum('nhd,khd->nhk', grad_att, val_parts, preferred_element_type=F32)  10.1 us
    reshape x3, local copies, waits for them, and re-layouts, to_units(): lanes = values.reshape(rows, columns // 128, 128).transpose(1, 0, 2)  7.83 us

profile of v1, /device:TPU:1, one launch (start us, length us, event | category | flops | bytes accessed | tf_op | source)
XLA Modules:
  0.0 274.9 jit_solution(8587156247447390608)
XLA Ops:
  0.6 1.6 copy-done
  2.2 4.6 %convolution_convert_fusion.1 = bf16[1024,512]{1,0:T(8,128)(2,1)S(1)} fusion(bf16[1024,2048]{1,0:T(8,128)(2,1)} %param.8, bf16[2048,512]{1,0:T(8,128)(2,1)S(1)} %copy-done), kind=kOutput, calls=%fused_computation.38 | convolution fusion | flops 2148007936 | bytes 7340032 | tf_op jit(solution)/shard_map/dot_general | solution.py:385
  6.8 1.0 copy-done.9
  7.8 0.5 fusion.60
  8.3 1.0 copy.33
  9.3 30.4 %shard_map.103 = f32[1024,128]{1,0:T(8,128)} custom-call(f32[1024,128]{1,0:T(8,128)} %bitcast.213), custom_call_target="tpu_custom_call" | custom-call | tf_op jit(solution)/shard_map/pallas_call | solution.py:144
  39.7 1.2 copy.34
  41.0 0.9 fusion.46
  41.9 1.3 copy.64
  43.2 1.7 convolution_convert_fusion
  44.9 3.6 %convolution_bitcast_fusion.1 = f32[32,16,8,128]{3,2,1,0:T(8,128)S(1)} fusion(bf16[256,1024]{1,0:T(8,128)(2,1)S(1)} %copy-done.28, bf16[1024,2048]{1,0:T(8,128)(2,1)} %param.8), kind=kOutput, calls=%fused_computation.29 | convolution fusion | flops 1073741824 | bytes 6815744 | tf_op jit(solution)/shard_map/dot_general | solution.py:435
  48.5 1.5 copy.74
  50.0 0.8 multiply_reduce_fusion.1
  50.8 1.0 fusion.27
  51.8 0.3 slice_add_fusion.2
  52.2 1.0 copy-done.5
  53.2 0.9 subtract_convert_fusion.1
  54.1 0.7 copy-done.16
  54.9 1.8 copy.35
  56.7 1.2 copy.38
  57.9 1.2 copy.36
  59.2 0.9 mul.91
  60.0 2.0 copy.54
  62.1 1.5 bitcast_reduce_fusion
  63.7 2.9 %fusion.14 = f32[8,64,256]{2,1,0:T(8,128)} fusion(bf16[1024,8,64]{0,2,1:T(8,128)(2,1)S(1)} %bitcast.208, f32[8,256,1024]{2,1,0:T(8,128)S(1)} %get-tuple-element.18, f32[1024,8]{0,1:T(8,128)S(1)} %get-tuple-element.17), kind=kOutput, calls=%fused_computation.23 | convolution fusion | flops 274726912 | bytes 9994240 | tf_op jit(solution)/shard_map/nhk,nhd->khd/dot_general | solution.py:419
  66.6 0.4 copy-done.2
  67.1 2.0 copy.47
  69.1 5.0 %fusion.24 = bf16[8,64,1024]{2,1,0:T(8,128)(2,1)S(1)} fusion(bf16[256,8,64]{0,2,1:T(8,128)(2,1)S(1)} %bitcast.226, f32[8,256,1024]{2,1,0:T(8,128)} %copy-done.2, f32[1024,8]{0,1:T(8,128)S(1)} %get-tuple-element.17), kind=kOutput, calls=%fused_computation.36 | convolution fusion | flops 275251200 | bytes 9732096 | tf_op jit(solution)/shard_map/nhk,khd->nhd/dot_general | solution.py:405
  74.2 1.7 fusion.61
  75.9 1.7 add_convert_fusion.1
  77.7 10.1 %convolution_bitcast_fusion = f32[1024,8,768]{0,2,1:T(8,128)} fusion(bf16[768,8,64]{0,2,1:T(8,128)(2,1)S(1)} %bitcast.198, bf16[1024,8,64]{0,2,1:T(8,128)(2,1)S(1)} %bitcast.209), kind=kOutput, calls=%fused_computation.1 | convolution fusion | flops 805306368 | bytes 27000832 | tf_op jit(solution)/shard_map/nhd,khd->nhk/dot_general | solution.py:417
  87.8 23.1 %fusion.6 = f32[8,64,256]{2,1,0:T(8,128)} fusion(f32[1024,512]{0,1:T(8,128)S(1)} %get-tuple-element.16, f32[1024,8]{0,1:T(8,128)S(1)} %add_rsqrt_fusion, f32[8,256,1024]{2,1,0:T(8,128)} %copy-done.2, f32[1024,8]{0,1:T(8,128)S(1)} %get-tuple-element.17, f32[1024,8,768]{0,2,1:T(8,128)} %convolution_bitcast_fusion), kind=kOutput, calls=%fused_computation.13 | convolution fusion | flops 296755456 | bytes 69828608 | tf_op jit(solution)/shard_map/nhk,nhd->khd/dot_general | solution.py:426
  110.9 25.8 %fusion.11 = (f32[1024,8]{0,1:T(8,128)S(1)}, f32[8,64,1024]{2,1,0:T(8,128)}) fusion(f32[1024,512]{0,1:T(8,128)S(1)} %get-tuple-element.16, f32[1024,8]{0,1:T(8,128)S(1)} %add_rsqrt_fusion, f32[1024,8]{0,1:T(8,128)S(1)} %get-tuple-element.17, f32[8,256,1024]{2,1,0:T(8,128)} %copy-done.2, f32[256,512]{0,1:T(8,128)S(1)} %copy.36, ...), kind=kOutput, calls=%fused_computation.18 | convolution fusion | flops 297533696 | bytes 71966720 | tf_op jit(solution)/shard_map/nhk,khd->nhd/dot_general | solution.py:425
  136.7 2.2 fusion.13
  139.0 1.7 fusion.34
  140.8 1.0 copy.45
  141.8 7.5 %fusion.36 = f32[512,2048]{1,0:T(8,128)} fusion(bf16[1024,2048]{1,0:T(8,128)(2,1)} %param.8, bf16[1024,512]{1,0:T(8,128)(2,1)S(1)} %copy-done.20, bf16[1024,512]{0,1:T(8,128)(2,1)} %bitcast.223, bf16[512,512]{1,0:T(8,128)(2,1)S(1)} %copy-done.26), kind=kOutput, calls=%fused_computation.55 | convolution fusion | flops 2685927424 | bytes 11010048 | tf_op jit(solution)/shard_map/dot_general | solution.py:29
  149.3 5.3 %copy.40 = f32[2048,4,128]{2,0,1:T(8,128)} copy(f32[2048,4,128]{0,2,1:T(8,128)} %bitcast.205) | data formatting | bytes 8388608 | tf_op jit(solution)/shard_map/reshape | solution.py:370
  154.6 4.7 %constant_dynamic-update-slice_fusion.5 = f32[18,1024,128]{2,1,0:T(8,128)} fusion(f32[8,1024,128]{2,1,0:T(8,128)} %bitcast.193), kind=kLoop, calls=%fused_computation.88 | loop fusion | bytes 8388608
  159.4 1.5 constant_dynamic-update-slice_fusion.4
  160.8 0.1 copy-done.23
  160.9 1.1 constant_dynamic-update-slice_fusion.3
  162.0 1.1 constant_dynamic-update-slice_fusion.2
  163.0 0.8 constant_dynamic-update-slice_fusion.1
  163.9 0.8 constant_dynamic-update-slice_fusion.in_ref
  164.7 75.9 %shard_map.104 = f32[18,1024,128]{2,1,0:T(8,128)} custom-call(f32[18,1024,128]{2,1,0:T(8,128)} %constant_dynamic-update-slice_fusion.in_ref), custom_call_target="tpu_custom_call" | custom-call | tf_op jit(solution)/shard_map/pallas_call | solution.py:348
  240.6 2.1 fusion.57
  242.8 0.2 copy.52
  243.2 1.0 copy.53
  244.2 1.4 fusion.44
  245.7 2.0 convolution_bitcast_fusion.2
  247.7 2.1 convolution_bitcast_fusion.3
  249.8 0.2 fusion.43
  250.0 2.1 fusion.18
  252.1 1.8 copy.49
  253.9 2.7 fusion.56
  256.6 2.2 slice-done.1
  258.8 0.7 copy-done.4
  259.5 6.5 %fusion.4 = f32[2048,512]{1,0:T(8,128)} fusion(f32[4,256,8,128]{3,2,1,0:T(8,128)S(1)} %bitcast.192, f32[256,2048]{0,1:T(8,128)S(1)} %bitcast.197, f32[768,512]{1,0:T(8,128)} %fusion.18), kind=kOutput, calls=%fused_computation.11 | convolution fusion | flops 3223584768 | bytes 12058624 | tf_op jit(solution)/shard_map/dot_general | solution.py:29
  266.0 0.7 copy.56
  266.7 1.4 stack_reshape.6
  268.1 0.7 copy.57
  268.8 1.4 stack_reshape.7
  270.2 4.7 %maximum_multiply_fusion = f32[4,512,512]{2,1,0:T(8,128)} fusion(f32[1,512,512]{2,1,0:T(8,128)} %stack_reshape.7, f32[1,512,512]{2,1,0:T(8,128)} %convolution_bitcast_fusion.2, f32[1,512,512]{2,1,0:T(8,128)} %convolution_bitcast_fusion.3, f32[1,512,512]{2,1,0:T(8,128)} %stack_reshape.6), kind=kLoop, calls=%fused_computation.12 | loop fusion | flops 4194304 | bytes 8388608 | tf_op jit(solution)/shard_map/mul | solution.py:463
  (83 shorter events, 0.6 us)
Async XLA Ops:
  0.6 1.6 copy-start
  2.2 5.6 %copy-start.28 = (bf16[256,1024]{1,0:T(8,128)(2,1)S(1)}, bf16[256,1024]{1,0:T(8,128)(2,1)}, u32[]{:S(2)}) copy-start(bf16[256,1024]{1,0:T(8,128)(2,1)} %param.14) | copy-start | bytes 1572868
  6.8 1.0 copy-start.9
  7.8 34.1 %copy-start.19 = (bf16[1024,512]{1,0:T(8,128)(2,1)S(1)}, bf16[1024,512]{1,0:T(8,128)(2,1)}, u32[]{:S(2)}) copy-start(bf16[1024,512]{1,0:T(8,128)(2,1)} %param.15) | copy-start | bytes 3145732
  7.8 35.4 %copy-start.32 = (bf16[512,512]{1,0:T(8,128)(2,1)S(1)}, bf16[512,512]{1,0:T(8,128)(2,1)}, u32[]{:S(2)}) copy-start(bf16[512,512]{1,0:T(8,128)(2,1)} %param.13) | copy-start | bytes 1572868
  44.9 5.1 %copy-start.10 = (bf16[1024,512]{1,0:T(8,128)(2,1)S(1)}, bf16[1024,512]{1,0:T(8,128)(2,1)}, u32[]{:S(2)}) copy-start(bf16[1024,512]{1,0:T(8,128)(2,1)} %copy-done.9) | copy-start | bytes 3145732
  44.9 5.1 %copy-start.25 = (bf16[512,512]{1,0:T(8,128)(2,1)S(1)}, bf16[512,512]{1,0:T(8,128)(2,1)}, u32[]{:S(2)}) copy-start(bf16[512,512]{1,0:T(8,128)(2,1)} %param.10) | copy-start | bytes 1572868
  48.4 2.4 copy-start.30
  48.5 2.4 copy-start.31
  48.5 2.4 copy-start.34
  48.5 2.3 copy-start.36
  52.2 1.0 copy-start.5
  54.1 0.7 copy-start.16
  62.1 1.6 copy-start.14
  63.6 3.4 %copy-start.2 = (f32[8,256,1024]{2,1,0:T(8,128)}, f32[8,256,1024]{2,1,0:T(8,128)S(1)}, u32[]{:S(2)}) copy-start(f32[8,256,1024]{2,1,0:T(8,128)S(1)} %get-tuple-element.18) | copy-start | bytes 25165828
  63.7 5.4 %copy-start.29 = (bf16[256,512]{0,1:T(8,128)(2,1)S(1)}, bf16[256,512]{0,1:T(8,128)(2,1)}, u32[]{:S(2)}) copy-start(bf16[256,512]{0,1:T(8,128)(2,1)} %copy.35) | copy-start | bytes 786436
  69.1 5.1 %copy-start.21 = (bf16[512,1024]{1,0:T(8,128)(2,1)S(1)}, bf16[512,1024]{1,0:T(8,128)(2,1)}, u32[]{:S(2)}) copy-start(bf16[512,1024]{1,0:T(8,128)(2,1)} %copy.64) | copy-start | bytes 3145732
  74.1 1.8 copy-start.11
  74.1 1.8 copy-start.33
  74.2 3.5 %copy-start.7 = (bf16[768,512]{0,1:T(8,128)(2,1)S(1)}, bf16[768,512]{0,1:T(8,128)(2,1)}, u32[]{:S(2)}) copy-start(bf16[768,512]{0,1:T(8,128)(2,1)} %copy.38) | copy-start | bytes 2359300
  74.2 3.5 %copy-start.15 = (bf16[1024,512]{0,1:T(8,128)(2,1)S(1)}, bf16[1024,512]{0,1:T(8,128)(2,1)}, u32[]{:S(2)}) copy-start(bf16[1024,512]{0,1:T(8,128)(2,1)} %convolution_convert_fusion) | copy-start | bytes 3145732
  136.7 2.3 copy-start.12
  139.0 1.8 copy-start.24
  139.0 1.8 copy-start.27
  139.0 2.8 %copy-start.20 = (bf16[1024,512]{1,0:T(8,128)(2,1)S(1)}, bf16[1024,512]{1,0:T(8,128)(2,1)}, u32[]{:S(2)}) copy-start(bf16[1024,512]{1,0:T(8,128)(2,1)} %param.15) | copy-start | bytes 3145732
  139.0 2.8 %copy-start.26 = (bf16[512,512]{1,0:T(8,128)(2,1)S(1)}, bf16[512,512]{1,0:T(8,128)(2,1)}, u32[]{:S(2)}) copy-start(bf16[512,512]{1,0:T(8,128)(2,1)} %param.10) | copy-start | bytes 1572868
  154.6 4.7 %copy-start.3 = (f32[32,16,8,128]{3,2,0,1:T(8,128)S(1)}, f32[32,16,8,128]{3,2,0,1:T(8,128)}, u32[]{:S(2)}) copy-start(f32[32,16,8,128]{3,2,0,1:T(8,128)} %copy.74) | copy-start | bytes 6291460
  159.3 1.6 copy-start.23
  159.3 2.6 copy-start.22
  159.4 3.7 %copy-start.18 = (f32[256,4,128]{2,0,1:T(8,128)S(1)}, f32[256,4,128]{2,0,1:T(8,128)}, u32[]{:S(2)}) copy-start(f32[256,4,128]{2,0,1:T(8,128)} %copy.45) | copy-start | bytes 1572868
  159.4 4.5 %copy-start.17 = (f32[256,4,128]{2,0,1:T(8,128)S(1)}, f32[256,4,128]{2,0,1:T(8,128)}, u32[]{:S(2)}) copy-start(f32[256,4,128]{2,0,1:T(8,128)} %copy.47) | copy-start | bytes 1572868
  240.6 3.5 %copy-start.6 = (f32[256,1024]{1,0:T(8,128)S(1)}, f32[256,1024]{1,0:T(8,128)}, u32[]{:S(2)}) copy-start(f32[256,1024]{1,0:T(8,128)} %copy-done.5) | copy-start | bytes 3145732
  243.1 2.5 copy-start.8
  245.6 4.3 %copy-start.35 = (bf16[512,512]{1,0:T(8,128)(2,1)S(1)}, bf16[512,512]{1,0:T(8,128)(2,1)}, u32[]{:S(2)}) copy-start(bf16[512,512]{1,0:T(8,128)(2,1)} %param.12) | copy-start | bytes 1572868
  245.6 4.3 %copy-start.37 = (bf16[512,512]{1,0:T(8,128)(2,1)S(1)}, bf16[512,512]{1,0:T(8,128)(2,1)}, u32[]{:S(2)}) copy-start(bf16[512,512]{1,0:T(8,128)(2,1)} %param.11) | copy-start | bytes 1572868
  250.0 2.2 slice-start
  256.6 2.2 slice-start.1
  256.6 2.9 %copy-start.4 = (f32[16,256,128]{1,2,0:T(8,128)S(1)}, f32[16,256,128]{1,2,0:T(8,128)}, u32[]{:S(2)}) copy-start(f32[16,256,128]{1,2,0:T(8,128)} %copy.49) | copy-start | bytes 6291460
  266.0 2.1 copy-start.13
  268.8 6.1 %copy-start.1 = (bf16[2048,512]{1,0:T(8,128)(2,1)S(1)}, bf16[2048,512]{1,0:T(8,128)(2,1)}, u32[]{:S(2)}) copy-start(bf16[2048,512]{1,0:T(8,128)(2,1)} %param.9) | copy-start | bytes 6291460

commit v2 on v0

v2 whole, which is shorter than its diff:
```python
import functools
import math

import jax
import jax.numpy as jnp
from jax import lax
from jax.experimental import pallas as pl
from jax.experimental.pallas import tpu as pltpu
from jax.sharding import PartitionSpec as P

MESH = pl.DeviceIdType.MESH
F32 = jnp.float32
BF16 = jnp.bfloat16
VMEM = pltpu.VMEM
ROWS = 1024
WIDTH = 512
LOOKBACK = 2048
KP = 256
PAIRS = 4
BLOCK = 256
BLOCKS = ROWS // BLOCK
NORM = 1.0 / math.sqrt(131072.0)
LAST_STAGE = 99


def dot(left, right, dims=((1,), (0,))):
    return lax.dot_general(left, right, (dims, ((), ())), preferred_element_type=F32)


def dot_t(left, right):
    return dot(left, right, ((1,), (1,)))


def hi_lo(values):
    upper = values.astype(BF16)
    return upper, (values - upper.astype(F32)).astype(BF16)


def rows(start, size, step=None):
    return pl.ds(pl.multiple_of(start, step or size), size)


def position():
    var = lax.axis_index("var")
    return {
        "x": lax.div(var, 8),
        "y": lax.rem(lax.div(var, 2), 4),
        "c": lax.rem(var, 2),
        "z": lax.axis_index("grp"),
    }


def moved(place, **steps):
    there = dict(place)
    for axis, step in steps.items():
        there[axis] = lax.rem(place[axis] + step, 2 if axis == "c" else 4)
    return (there["x"] * 8 + there["y"] * 2 + there["c"], there["z"])


class Copies:
    def __init__(self, send, recv):
        self.send, self.recv = send, recv
        self.count = 0
        self.waiting = []

    def __call__(self, src, dst, device):
        slot = self.count
        self.count += 1
        made = pltpu.make_async_remote_copy(
            src_ref=src,
            dst_ref=dst,
            send_sem=self.send.at[slot],
            recv_sem=self.recv.at[slot],
            device_id=device,
            device_id_type=MESH,
        )
        made.start()
        self.waiting.append(made)
        return made

    def drain(self):
        for made in self.waiting:
            made.wait_send()
        self.waiting = []


X, Y, Z = ("x", "y", "z"), ("y", "z", "x"), ("z", "x", "y")


class Sum:
    def __init__(self, here, copies, groups, bufs):
        self.here, self.copy, self.groups = here, copies, groups
        self.data, self.half, self.one, self.two, self.three, self.out = bufs
        self.base = here["c"] * 512
        self.across = []
        self.made = {}

    def core(self, group):
        _, start, size = self.groups[group]
        units = pl.ds(start, size)
        self.across.append(
            self.copy(
                self.data.at[units, rows((1 - self.here["c"]) * 512, 512)],
                self.half.at[units],
                moved(self.here, c=1),
            )
        )

    def place(self, group, level):
        order = self.groups[group][0]
        sizes = (128, 32, 8)
        at = self.base
        for axis, size in zip(order[:level], sizes[:level]):
            at = at + self.here[axis] * size
        return at

    def scatter(self, level, group):
        order, start, size = self.groups[group]
        axis = order[level]
        extent = (128, 32, 8)[level]
        buffer = (self.one, self.two, self.three)[level]
        at = self.place(group, level)
        self.made[group] = [
            self.copy(
                self.data.at[
                    pl.ds(start, size),
                    rows(at + lax.rem(self.here[axis] + step, 4) * extent, extent),
                ],
                buffer.at[step - 1, pl.ds(start, size)],
                moved(self.here, **{axis: step}),
            )
            for step in (2, 1, 3)
        ]

    def gather(self, level, group):
        order, start, size = self.groups[group]
        axis = order[level]
        extent = (128, 32, 8)[level]
        own = self.out.at[pl.ds(start, size), rows(self.place(group, level + 1), extent)]
        self.made[group] = [
            self.copy(own, own, moved(self.here, **{axis: step})) for step in (2, 1, 3)
        ]
        return own

    def step1(self):
        for group, (_, start, size) in enumerate(self.groups):
            self.across[group].wait_recv()

            @pl.loop(start, start + size)
            def _(unit):
                where = (unit, rows(self.base, 512))
                self.data[where] = self.data[where] + self.half[unit]

            self.scatter(0, group)

    def reduced(self, level, group):
        _, start, size = self.groups[group]
        extent = (128, 32, 8)[level]
        buffer = (self.one, self.two, self.three)[level]
        for made in self.made[group]:
            made.wait_recv()
        units = pl.ds(start, size)
        where = (units, rows(self.place(group, level + 1), extent))
        total = (self.data[where] + buffer[0, units]) + (buffer[1, units] + buffer[2, units])
        if level == 2:
            self.out[where] = total
        else:
            self.data[where] = total

    def step2(self):
        for group in range(len(self.groups)):
            self.reduced(0, group)
            self.scatter(1, group)

    def step3(self):
        for group in range(len(self.groups)):
            self.reduced(1, group)
            self.scatter(2, group)

    def step4(self):
        for group in range(len(self.groups)):
            self.reduced(2, group)
            self.gather(2, group)

    def gathered(self, group):
        for made in self.made[group]:
            made.wait_recv()

    def step5(self):
        for group in range(len(self.groups)):
            self.gathered(group)
            self.gather(1, group)

    def step6(self):
        self.passed = []
        for group in range(len(self.groups)):
            self.gathered(group)
            own = self.gather(0, group)
            self.passed.append([self.copy(own, own, moved(self.here, c=1))])

    def step7(self):
        for group, (order, start, size) in enumerate(self.groups):
            for made, step in zip(self.made[group], (2, 1, 3)):
                made.wait_recv()
                chunk = lax.rem(self.here[order[0]] + 4 - step, 4)
                piece = self.out.at[pl.ds(start, size), rows(self.base + chunk * 128, 128)]
                self.passed[group].append(self.copy(piece, piece, moved(self.here, c=1)))

    def step8(self, group):
        for made in self.passed[group]:
            made.wait_recv()

    def all8(self):
        for group in range(len(self.groups)):
            self.step8(group)


def sum_bufs(units):
    return [
        VMEM((units, 1024, 128), F32),
        VMEM((units, 512, 128), F32),
        VMEM((3, units, 128, 128), F32),
        VMEM((3, units, 32, 128), F32),
        VMEM((3, units, 8, 128), F32),
        VMEM((units, 1024, 128), F32),
    ]


S_GROUPS = ((X, 0, 1), (Y, 1, 2), (Z, 3, 1))
Q_GROUPS = ((X, 0, 1), (Y, 1, 1), (Z, 2, 1))
E_GROUPS = (((X, 0, 2), (Y, 2, 1), (Z, 3, 1)), ((Z, 0, 2), (Y, 2, 1), (X, 3, 1)))

SHAPES = dict(
    series=((ROWS, LOOKBACK), BF16),
    w_embed=((LOOKBACK, WIDTH), BF16),
    w_query=((WIDTH, WIDTH), BF16),
    w_key=((WIDTH, WIDTH), BF16),
    w_value=((WIDTH, WIDTH), BF16),
    w_out=((WIDTH, WIDTH), BF16),
    proj=((KP, ROWS), BF16),
    cot=((ROWS, WIDTH), BF16),
    series_t=((LOOKBACK, ROWS), BF16),
    hid=((ROWS, WIDTH), BF16),
    hid_t=((WIDTH, ROWS), BF16),
    q_r=((PAIRS, ROWS, 128), F32),
    q_n=((PAIRS, ROWS, 128), BF16),
    g_att=((PAIRS, ROWS, 128), BF16),
    att=((PAIRS, ROWS, 128), BF16),
    g_query=((PAIRS, ROWS, 128), BF16),
    g_hid=((ROWS, WIDTH), BF16),
    key_n=((PAIRS, KP, 128), F32),
    key_r=((PAIRS, KP, 128), F32),
    key_in=((PAIRS, 128, 512), BF16),
    key_out=((PAIRS, 512, 128), BF16),
    val_in=((PAIRS, 256, 512), BF16),
    val_out=((PAIRS, 512, 128), BF16),
    ph_in=((1024, 128), F32),
    ph_half=((512, 128), F32),
    ph_core=((512, 128), F32),
    ph_plane=((16, 32, 128), F32),
    ph_x=((4, 32, 128), F32),
    ph=((1024, 128), F32),
    ph_t=((2, WIDTH, KP), BF16),
    gk=((2, KP, WIDTH), BF16),
    gv=((2, KP, WIDTH), BF16),
    back=((2, KP, WIDTH), BF16),
    out=((ROWS, WIDTH), BF16),
)
LOADS = ("w_embed", "proj", "cot", "w_out", "w_query", "w_key", "w_value")
N_COPIES = 50 + 5 * 3 * 23


def layer_kernel(*refs):
    names = ("series", "w_embed", "w_query", "w_key", "w_value", "w_out", "proj", "cot")
    hbm = dict(zip(names, refs[:8]))
    out_hbm, embed_hbm, attn_hbm = refs[8:11]
    refs = refs[11:]
    v = dict(zip(SHAPES, refs[: len(SHAPES)]))
    refs = refs[len(SHAPES) :]
    s_bufs, q0_bufs, q1_bufs, e0_bufs, e1_bufs = (refs[6 * i : 6 * i + 6] for i in range(5))
    send, recv, load_sem, store_sem = refs[30:]
    here = position()
    core, plane = here["c"], here["y"] * 4 + here["z"]
    base = core * 512

    def plane_device(step):
        there = lax.rem(plane + step, 16)
        return (here["x"] * 8 + lax.div(there, 4) * 2 + core, lax.rem(there, 4))

    loads = {}
    for slot, name in enumerate(LOADS):
        loads[name] = pltpu.make_async_copy(hbm[name], v[name], load_sem.at[slot])
    series_loads = []
    for block in range(BLOCKS):
        where = pl.ds(block * BLOCK, BLOCK)
        series_loads.append(
            pltpu.make_async_copy(
                hbm["series"].at[where], v["series"].at[where], load_sem.at[len(LOADS) + block]
            )
        )
    loads["w_embed"].start()
    for made in series_loads:
        made.start()
    for name in LOADS[1:]:
        loads[name].start()

    barrier = pltpu.get_barrier_semaphore()
    others = [moved(here, c=1)]
    others += [moved(here, x=step) for step in (1, 2, 3)]
    others += [plane_device(step) for step in range(1, 16)]
    for device in others:
        pl.semaphore_signal(barrier, inc=1, device_id=device, device_id_type=MESH)

    copies = Copies(send, recv)
    sum_s = Sum(here, copies, S_GROUPS, s_bufs)
    sum_q = [Sum(here, copies, Q_GROUPS, bufs) for bufs in (q0_bufs, q1_bufs)]
    sum_e = [Sum(here, copies, E_GROUPS[i], bufs) for i, bufs in enumerate((e0_bufs, e1_bufs))]

    lane = lax.broadcasted_iota(jnp.int32, (256, 128), 1) & 64
    row = lax.broadcasted_iota(jnp.int32, (256, 128), 0) & 64
    ones = jnp.where(lane == row, 1.0 / 64, 0.0).astype(BF16)

    def head_mean(values):
        return dot(jnp.concatenate(hi_lo(values), 1), ones)

    loads["w_embed"].wait()
    for block in range(BLOCKS):
        series_loads[block].wait()
        where = pl.ds(block * BLOCK, BLOCK)
        v["hid"][where] = dot(v["series"][where], v["w_embed"][...]).astype(BF16)
    loads["proj"].wait()
    part = dot(v["proj"][...], v["hid"][...])
    for pair in range(PAIRS):
        v["ph_in"][pl.ds(pair * 256, 256)] = part[:, pair * 128 : pair * 128 + 128]

    pl.semaphore_wait(barrier, len(others))
    across = copies(v["ph_in"].at[rows((1 - core) * 512, 512)], v["ph_core"], moved(here, c=1))

    loads["cot"].wait()
    loads["w_out"].wait()

    @pl.loop(0, BLOCKS)
    def _(block):
        where = rows(block * BLOCK, BLOCK)
        grad = dot_t(v["cot"][where], v["w_out"][...]).astype(BF16)
        for pair in range(PAIRS):
            v["g_att"][pair, where] = grad[:, pair * 128 : pair * 128 + 128]

    across.wait_recv()
    v["ph_half"][...] = v["ph_in"][rows(base, 512)] + v["ph_core"][...]
    scattered = []
    for step in range(1, 16):
        there = lax.rem(plane + step, 16)
        scattered.append(
            copies(v["ph_half"].at[rows(there * 32, 32)], v["ph_plane"].at[step], plane_device(step))
        )

    loads["w_query"].wait()

    @pl.loop(0, BLOCKS)
    def _(block):
        where = rows(block * BLOCK, BLOCK)
        query = dot(v["hid"][where], v["w_query"][...])
        for pair in range(PAIRS):
            part = query[:, pair * 128 : pair * 128 + 128]
            factor = lax.rsqrt(head_mean(part * part) + 1e-06)
            v["q_r"][pair, where] = factor
            v["q_n"][pair, where] = (part * factor).astype(BF16)

    own = pl.multiple_of(plane * 32, 32)
    for made in scattered:
        made.wait_recv()
    total = v["ph_half"][pl.ds(own, 32)]
    for step in range(1, 16):
        total = total + v["ph_plane"][step]
    v["ph_x"][here["x"]] = total
    mine = v["ph_x"].at[here["x"]]
    shares = [copies(mine, mine, moved(here, x=step)) for step in (2, 1, 3)]

    @pl.loop(0, 4)
    def _(part):
        where = rows(part * 256, 256)
        v["series_t"][where] = v["series"][:, where].T

    for made in shares:
        made.wait_recv()
    whole = (v["ph_x"][0] + v["ph_x"][1]) + (v["ph_x"][2] + v["ph_x"][3])
    mine = v["ph"].at[rows(base + own, 32)]
    mine[...] = whole
    spread = [copies(mine, mine, plane_device(step)) for step in range(1, 16)]
    passed = [copies(mine, mine, moved(here, c=1))]

    @pl.loop(4, 8)
    def _(part):
        where = rows(part * 256, 256)
        v["series_t"][where] = v["series"][:, where].T

    v["hid_t"][...] = v["hid"][...].T

    for step in range(1, 16):
        spread[step - 1].wait_recv()
        origin = lax.rem(plane + 16 - step, 16)
        piece = v["ph"].at[rows(base + origin * 32, 32)]
        passed.append(copies(piece, piece, moved(here, c=1)))

    @pl.loop(0, 8)
    def _(part):
        got = dot_t(v["series_t"][rows(part * 256, 256)], v["proj"][...])
        unit = lax.div(part, 4) * 2
        where = rows(lax.rem(part, 4) * 256, 256)
        sum_s.data[unit, where] = got[:, :128]
        sum_s.data[unit + 1, where] = got[:, 128:]

    for made in passed:
        made.wait_recv()
    for group in range(3):
        sum_s.core(group)

    loads["w_key"].wait()
    loads["w_value"].wait()
    ph = jnp.concatenate([v["ph"][pl.ds(pair * 256, 256)] for pair in range(PAIRS)], 1)
    ph_hi, ph_lo = hi_lo(ph)
    low_half = lax.broadcasted_iota(jnp.int32, (256, 128), 1) < 64
    none = jnp.zeros((256, 128), BF16)
    keys = dot(ph_hi, v["w_key"][...]) + dot(ph_lo, v["w_key"][...])
    values = dot(ph_hi, v["w_value"][...]) + dot(ph_lo, v["w_value"][...])
    blank = jnp.zeros((64, 256), BF16)
    for pair in range(PAIRS):
        part = keys[:, pair * 128 : pair * 128 + 128]
        factor = lax.rsqrt(head_mean(part * part) + 1e-06)
        normed = part * factor
        v["key_n"][pair] = normed
        v["key_r"][pair] = factor
        eighth = (normed * 0.125).astype(BF16)
        v["key_out"][pair, :256] = jnp.where(low_half, eighth, none)
        v["key_out"][pair, 256:] = jnp.where(low_half, none, eighth)
        turned = eighth.T
        v["key_in"][pair, :64, :256] = turned[:64]
        v["key_in"][pair, 64:, 256:] = turned[64:]
        v["key_in"][pair, :64, 256:] = blank
        v["key_in"][pair, 64:, :256] = blank
        val_hi, val_lo = hi_lo(values[:, pair * 128 : pair * 128 + 128])
        v["val_out"][pair, :256] = jnp.where(low_half, val_hi, none)
        v["val_out"][pair, 256:] = jnp.where(low_half, none, val_hi)
        for index, value in enumerate((val_hi, val_lo)):
            turned = value.T
            at = index * 128
            v["val_in"][pair, at : at + 64, :256] = turned[:64]
            v["val_in"][pair, at + 64 : at + 128, 256:] = turned[64:]
            v["val_in"][pair, at : at + 64, 256:] = blank
            v["val_in"][pair, at + 64 : at + 128, :256] = blank

    def attention(pair):
        sums = sum_q[pair // 2].data
        first = (pair % 2) * 128
        for part in range(4):
            sums[0, pl.ds(part * 256 + first, 128)] = jnp.zeros((128, 128), F32)

        @pl.loop(0, BLOCKS)
        def _(block):
            where = rows(block * BLOCK, BLOCK)
            query = v["q_n"][pair, where]
            grad = v["g_att"][pair, where]
            scores = dot(query, v["key_in"][pair])
            grad_probs = dot(jnp.concatenate([grad, grad], 1), v["val_in"][pair])
            query_t, grad_t = query.T, grad.T
            probs_b, grad_scores = [], []
            for head in range(2):
                lanes = slice(head * 256, head * 256 + 256)
                expo = jnp.exp(scores[:, lanes])
                probs = expo * (1.0 / jnp.sum(expo, axis=1, keepdims=True))
                grad_p = grad_probs[:, lanes]
                inner = jnp.sum(probs * grad_p, axis=1, keepdims=True)
                probs_b.append(probs.astype(BF16))
                grad_scores.append((probs * (grad_p - inner)).astype(BF16))
                for at, got in (
                    (0, dot(query_t[head * 64 : head * 64 + 64], grad_scores[head])),
                    (512, dot(grad_t[head * 64 : head * 64 + 64], probs_b[head])),
                ):
                    for side in range(2):
                        rest = pl.ds(at + side * 256 + first + head * 64, 64)
                        sums[0, rest] = sums[0, rest] + got[:, side * 128 : side * 128 + 128]
            attended = dot(jnp.concatenate(probs_b, 1), v["val_out"][pair])
            v["att"][pair, where] = attended.astype(BF16)
            grad_n = dot(jnp.concatenate(grad_scores, 1), v["key_out"][pair])
            normed = query.astype(F32)
            grad_q = v["q_r"][pair, where] * (grad_n - normed * head_mean(grad_n * normed))
            v["g_query"][pair, where] = grad_q.astype(BF16)

    def weight_grads(quad):
        both = (2 * quad, 2 * quad + 1)
        sums = sum_q[quad].data
        att = jnp.concatenate([v["att"][pair] for pair in both], 1)
        got = dot(att.T, v["cot"][...])
        for part in range(4):
            sums[2, pl.ds(part * 256, 256)] = got[:, part * 128 : part * 128 + 128]
        sum_q[quad].core(0)
        got = dot(v["hid_t"][...], jnp.concatenate([v["g_query"][pair] for pair in both], 1))
        for part in range(2):
            sums[1, pl.ds(part * 512, 512)] = got[:, part * 128 : part * 128 + 128]
        sum_q[quad].core(1)
        sum_q[quad].core(2)

    attention(0)
    sum_s.step1()
    attention(1)
    sum_s.step2()
    weight_grads(0)
    sum_s.step3()
    attention(2)
    sum_q[0].step1()
    sum_s.step4()
    attention(3)
    sum_q[0].step2()
    sum_s.step5()

    @pl.loop(0, BLOCKS)
    def _(block):
        where = rows(block * BLOCK, BLOCK)
        grad = jnp.concatenate([v["g_query"][pair, where] for pair in range(PAIRS)], 1)
        v["g_hid"][where] = (
            v["cot"][where].astype(F32) + dot_t(grad, v["w_query"][...])
        ).astype(BF16)

    weight_grads(1)
    sum_q[0].step3()
    sum_s.step6()

    def embed_part(index):
        @pl.loop(0, 4)
        def _(part):
            got = dot(v["series_t"][rows(index * 1024 + part * 256, 256)], v["g_hid"][...])
            where = rows(part * 256, 256)
            for unit in range(4):
                sum_e[index].data[unit, where] = got[:, unit * 128 : unit * 128 + 128]

        for group in range(3):
            sum_e[index].core(group)

    embed_part(0)
    sum_q[1].step1()
    embed_part(1)
    sum_e[0].step1()
    sum_q[0].step4()
    sum_s.step7()
    sum_q[1].step2()
    sum_e[1].step1()
    sum_q[0].step5()
    sum_q[1].step3()
    sum_e[0].step2()

    @pl.loop(0, BLOCKS)
    def _(block):
        where = rows(block * BLOCK, BLOCK)
        att = jnp.concatenate([v["att"][pair, where] for pair in range(PAIRS)], 1)
        v["out"][where] = (v["hid"][where].astype(F32) + dot(att, v["w_out"][...])).astype(BF16)

    stores = []

    def store(src, dst):
        made = pltpu.make_async_copy(src, dst, store_sem.at[len(stores)])
        made.start()
        stores.append(made)

    store(v["out"], out_hbm)
    sum_q[0].step6()
    sum_q[1].step4()
    sum_e[1].step2()
    sum_e[0].step3()
    sum_q[1].step5()
    sum_q[0].step7()
    sum_e[1].step3()
    sum_e[0].step4()
    sum_q[1].step6()
    sum_e[1].step4()
    sum_e[0].step5()
    sum_q[0].all8()
    sum_s.all8()
    sum_q[1].step7()
    sum_e[1].step5()
    sum_e[0].step6()
    for side, part in enumerate(hi_lo(ph)):
        v["ph_t"][side] = part.T
    sum_e[1].step6()
    sum_q[1].all8()
    copies.drain()

    for quad in range(2):
        for half in range(2):
            pair = quad * 2 + half
            lanes = pl.ds(pair * 128, 128)
            turned = []
            for at in (0, 512):
                turned.append(
                    jnp.concatenate(
                        [
                            sum_q[quad].out[0, pl.ds(at + side * 256 + half * 128, 128)]
                            for side in range(2)
                        ],
                        1,
                    ).T
                )
            grad_n = turned[0] * 0.125
            normed = v["key_n"][pair]
            grad_k = v["key_r"][pair] * (grad_n - normed * head_mean(grad_n * normed))
            for index, (name, value) in enumerate((("gk", grad_k), ("gv", turned[1]))):
                for side, part in enumerate(hi_lo(value)):
                    v[name][side, :, lanes] = part
    back = dot_t(v["gk"][0], v["w_key"][...]) + dot_t(v["gk"][1], v["w_key"][...])
    back = back + dot_t(v["gv"][0], v["w_value"][...]) + dot_t(v["gv"][1], v["w_value"][...])
    for side, part in enumerate(hi_lo(back)):
        v["back"][side] = part
    for index, name in enumerate(("gk", "gv")):
        got = dot(v["ph_t"][0], v[name][0]) + dot(v["ph_t"][0], v[name][1])
        got = (got + dot(v["ph_t"][1], v[name][0])) * NORM
        for part in range(4):
            sum_s.data[
                index * 2 + part // 2, pl.ds((part % 2) * 512, 512)
            ] = got[:, part * 128 : part * 128 + 128]
            store(
                sum_s.data.at[index * 2 + part // 2, pl.ds((part % 2) * 512, 512)],
                attn_hbm.at[1 + index, :, pl.ds(part * 128, 128)],
            )
    for quad in range(2):
        out = sum_q[quad].out

        @pl.loop(1, 3)
        def _(unit):
            out[unit] = out[unit] * NORM

        for part in range(2):
            store(
                out.at[1, pl.ds(part * 512, 512)],
                attn_hbm.at[0, :, pl.ds(quad * 256 + part * 128, 128)],
            )
        for part in range(4):
            store(
                out.at[2, pl.ds(part * 256, 256)],
                attn_hbm.at[3, pl.ds(quad * 256, 256), pl.ds(part * 128, 128)],
            )
    sum_e[0].step7()
    sum_e[1].step7()
    for index in range(2):

        @pl.loop(0, 4)
        def _(part):
            where = rows(part * 256, 256)
            left = jnp.concatenate([sum_s.out[index * 2 + side, where] for side in range(2)], 1)
            left_hi, left_lo = hi_lo(left)
            got = dot(left_hi, v["back"][0]) + dot(left_hi, v["back"][1])
            got = got + dot(left_lo, v["back"][0])
            for unit in range(4):
                sum_e[index].data[unit, where] = got[:, unit * 128 : unit * 128 + 128]

    for index in range(2):
        for group, (_, start, size) in enumerate(E_GROUPS[index]):
            sum_e[index].step8(group)
            if group == 2:
                copies.drain()
        for unit in range(4):

            @pl.loop(0, 4)
            def _(part):
                where = (unit, rows(part * 256, 256))
                sum_e[index].out[where] = (
                    sum_e[index].out[where] + sum_e[index].data[where]
                ) * NORM

            store(
                sum_e[index].out.at[unit],
                embed_hbm.at[pl.ds(index * 1024, 1024), pl.ds(unit * 128, 128)],
            )
    copies.drain()
    for made in stores:
        made.wait()


def local(series, w_embed, w_query, w_key, w_value, w_out, proj, cotangent):
    anywhere = pl.BlockSpec(memory_space=pl.ANY)
    return pl.pallas_call(
        layer_kernel,
        out_shape=(
            jax.ShapeDtypeStruct((ROWS, WIDTH), BF16),
            jax.ShapeDtypeStruct((LOOKBACK, WIDTH), F32),
            jax.ShapeDtypeStruct((4, WIDTH, WIDTH), F32),
        ),
        in_specs=[anywhere] * 8,
        out_specs=(anywhere,) * 3,
        scratch_shapes=[VMEM(shape, dtype) for shape, dtype in SHAPES.values()]
        + sum_bufs(4)
        + sum_bufs(3) * 2
        + sum_bufs(4) * 2
        + [
            pltpu.SemaphoreType.DMA((N_COPIES,)),
            pltpu.SemaphoreType.DMA((N_COPIES,)),
            pltpu.SemaphoreType.DMA((len(LOADS) + BLOCKS,)),
            pltpu.SemaphoreType.DMA((32,)),
        ],
        compiler_params=pltpu.CompilerParams(
            collective_id=0, has_side_effects=True, vmem_limit_bytes=63 * 1024 * 1024
        ),
    )(series, w_embed, w_query, w_key, w_value, w_out, proj, cotangent)


def solution(mesh):
    return jax.shard_map(
        local,
        mesh=mesh,
        in_specs=(
            P(("var", "grp"), None),
            P(),
            P(),
            P(),
            P(),
            P(),
            P(None, ("var", "grp")),
            P(("var", "grp"), None),
        ),
        out_specs=(P(("var", "grp"), None), P(), P()),
        check_vma=False,
    )
```

time: 610 us -> 126 us (0.21)
  waiting for transfers between devices: 444 us -> 0 us
  Pallas kernels: 0 us -> 115 us
  matrix products: 110 us -> 0 us
  other arithmetic: 24.5 us -> 0 us
  between operations: 14.1 us -> 0.64 us
  local copies, waits for them, and re-layouts: 16.3 us -> 9.1 us
    psum x3 -> x0, waiting for transfers between devices: 444 us -> none  [the longest x1 158 us: weight_totals(): return lax.psum((embed_part, attn_part), ('var', 'grp'))]
    pallas_call x0 -> x1, Pallas kernels: none -> 115 us  [local(): pl.pallas_call(layer_kernel, out_shape=(jax.ShapeDtypeStruct((ROWS, WIDTH...]
    dot_general x18 -> x0, matrix products: 110 us -> none  [the longest x1 25.8 us: local(): jnp.einsum('nhk,khd->nhd', grad_scores, key_nb, preferred_element_type=jn...]
    mul x3 -> x0, other arithmetic: 10.9 us -> none  [the longest x1 4.95 us: local(): return (output, embed_sum * norm, grad_attn)]
    convert_element_type x6 -> x0, other arithmetic: 7.73 us -> none  [the longest x2 3.11 us: split_parts(): upper = values.astype(jnp.bfloat16)]
    unnamed x49 -> x5, local copies, waits for them, and re-layouts: 15.1 us -> 9.1 us
  transfers between devices with their start and end apart: 3 -> 0, of which waited for: 3 -> 0; matrix products, arithmetic and copies ran while one was open for 2% -> 0% of each run, Pallas kernels for 0% -> 0%
where the time goes in v2:
time: 126 us; the launch traced here: 125 us
  Pallas kernels  115 us (91%)
  local copies, waits for them, and re-layouts  9.1 us (7%)
    pallas_call x1, Pallas kernels, local(): pl.pallas_call(layer_kernel, out_shape=(jax.ShapeDtypeStruct((ROWS, WIDTH...  115 us
    unnamed x5, local copies, waits for them, and re-layouts  9.1 us

profile of v2, /device:TPU:1, one launch (start us, length us, event | category | flops | bytes accessed | tf_op | source)
XLA Modules:
  0.0 124.9 jit_solution(3190722862844761001)
XLA Ops:
  0.6 115.2 %shard_map.103 = (bf16[1024,512]{1,0:T(8,128)(2,1)}, f32[2048,512]{1,0:T(8,128)}, f32[4,512,512]{2,1,0:T(8,128)}) custom-call(bf16[1024,2048]{1,0:T(8,128)(2,1)} %refs_0_.1, bf16[2048,512]{1,0:T(8,128)(2,1)} %refs_1_.1, bf16[512,512]{1,0:T(8,128)(2,1)} %refs_2_.1, bf16[512,512]{1,0:T(8,128)(2,1)} %refs_3_.1, bf16[512,512]{1,0:T(8,128)(2,1)} %refs_4_.1, ...), custom_call_target="tpu_custom_call" | custom-call | tf_op jit(solution)/shard_map/pallas_call | solution.py:680
  115.8 2.3 %copy.14 = bf16[1024,512]{1,0:T(8,128)(2,1)} copy(bf16[1024,512]{1,0:T(8,128)(2,1)} %get-tuple-element.6) | data formatting | bytes 2097152
  118.1 0.0 copy-start
  118.1 4.8 %copy.15 = f32[2048,512]{1,0:T(8,128)} copy(f32[2048,512]{1,0:T(8,128)} %get-tuple-element.7) | data formatting | bytes 8388608
  122.9 0.0 copy-done
  122.9 2.0 %copy.16 = f32[4,512,512]{2,1,0:T(8,128)} copy(f32[4,512,512]{2,1,0:T(8,128)S(1)} %copy-done) | data formatting | bytes 8388608
Async XLA Ops:
  118.1 4.8 %copy-start = (f32[4,512,512]{2,1,0:T(8,128)S(1)}, f32[4,512,512]{2,1,0:T(8,128)}, u32[]{:S(2)}) copy-start(f32[4,512,512]{2,1,0:T(8,128)} %get-tuple-element.8) | copy-start | bytes 12582916

commit v3 on v2

--- a/solution.py
+++ b/solution.py
@@ -20,7 +20,6 @@
 BLOCK = 256
 BLOCKS = ROWS // BLOCK
 NORM = 1.0 / math.sqrt(131072.0)
-LAST_STAGE = 99
 
 
 def dot(left, right, dims=((1,), (0,))):
@@ -78,10 +77,10 @@
         self.waiting.append(made)
         return made
 
-    def drain(self):
-        for made in self.waiting:
+    def drain(self, first=None):
+        for made in self.waiting[:first]:
             made.wait_send()
-        self.waiting = []
+        self.waiting = self.waiting[len(self.waiting) if first is None else first :]
 
 
 X, Y, Z = ("x", "y", "z"), ("y", "z", "x"), ("z", "x", "y")
@@ -94,6 +93,7 @@
         self.base = here["c"] * 512
         self.across = []
         self.made = {}
+        self.sends = []
 
     def core(self, group):
         _, start, size = self.groups[group]
@@ -105,10 +105,11 @@
                 moved(self.here, c=1),
             )
         )
+        self.sends.append(self.across[-1])
 
     def place(self, group, level):
         order = self.groups[group][0]
-        sizes = (128, 32, 8)
+        sizes = (128, 32)
         at = self.base
         for axis, size in zip(order[:level], sizes[:level]):
             at = at + self.here[axis] * size
@@ -117,8 +118,8 @@
     def scatter(self, level, group):
         order, start, size = self.groups[group]
         axis = order[level]
-        extent = (128, 32, 8)[level]
-        buffer = (self.one, self.two, self.three)[level]
+        extent = (128, 32)[level]
+        buffer = (self.one, self.two)[level]
         at = self.place(group, level)
         self.made[group] = [
             self.copy(
@@ -131,11 +132,19 @@
             )
             for step in (2, 1, 3)
         ]
+        self.sends += self.made[group]
+
+    def settle(self):
+        for made in self.sends:
+            made.wait_send()
+        self.copy.waiting = [
+            made for made in self.copy.waiting if not any(made is one for one in self.sends)
+        ]
 
     def gather(self, level, group):
         order, start, size = self.groups[group]
         axis = order[level]
-        extent = (128, 32, 8)[level]
+        extent = (128, 32)[level]
         own = self.out.at[pl.ds(start, size), rows(self.place(group, level + 1), extent)]
         self.made[group] = [
             self.copy(own, own, moved(self.here, **{axis: step})) for step in (2, 1, 3)
@@ -154,18 +163,27 @@
             self.scatter(0, group)
 
     def reduced(self, level, group):
-        _, start, size = self.groups[group]
-        extent = (128, 32, 8)[level]
-        buffer = (self.one, self.two, self.three)[level]
+        order, start, size = self.groups[group]
+        extent = (128, 32)[level]
+        buffer = (self.one, self.two)[level]
         for made in self.made[group]:
             made.wait_recv()
         units = pl.ds(start, size)
         where = (units, rows(self.place(group, level + 1), extent))
         total = (self.data[where] + buffer[0, units]) + (buffer[1, units] + buffer[2, units])
-        if level == 2:
-            self.out[where] = total
+        if level == 0:
+            self.data[where] = total
         else:
-            self.data[where] = total
+            mine = (self.here[order[2]], units)
+            self.three[mine] = total
+            self.made[group] = [
+                self.copy(
+                    self.three.at[mine],
+                    self.three.at[mine],
+                    moved(self.here, **{order[2]: step}),
+                )
+                for step in (2, 1, 3)
+            ]
 
     def step2(self):
         for group in range(len(self.groups)):
@@ -175,30 +193,28 @@
     def step3(self):
         for group in range(len(self.groups)):
             self.reduced(1, group)
-            self.scatter(2, group)
 
     def step4(self):
-        for group in range(len(self.groups)):
-            self.reduced(2, group)
-            self.gather(2, group)
+        for group, (_, start, size) in enumerate(self.groups):
+            self.gathered(group)
+            units = pl.ds(start, size)
+            part = [self.three[index, units] for index in range(4)]
+            where = (units, rows(self.place(group, 2), 32))
+            self.out[where] = (part[0] + part[1]) + (part[2] + part[3])
+            self.gather(1, group)
 
     def gathered(self, group):
         for made in self.made[group]:
             made.wait_recv()
 
     def step5(self):
-        for group in range(len(self.groups)):
-            self.gathered(group)
-            self.gather(1, group)
-
-    def step6(self):
         self.passed = []
         for group in range(len(self.groups)):
             self.gathered(group)
             own = self.gather(0, group)
             self.passed.append([self.copy(own, own, moved(self.here, c=1))])
 
-    def step7(self):
+    def step6(self):
         for group, (order, start, size) in enumerate(self.groups):
             for made, step in zip(self.made[group], (2, 1, 3)):
                 made.wait_recv()
@@ -206,24 +222,23 @@
                 piece = self.out.at[pl.ds(start, size), rows(self.base + chunk * 128, 128)]
                 self.passed[group].append(self.copy(piece, piece, moved(self.here, c=1)))
 
-    def step8(self, group):
+    def step7(self, group):
         for made in self.passed[group]:
             made.wait_recv()
 
-    def all8(self):
+    def all7(self):
         for group in range(len(self.groups)):
-            self.step8(group)
-
-
-def sum_bufs(units):
+            self.step7(group)
+
+
+def sum_bufs(units, out=True):
     return [
         VMEM((units, 1024, 128), F32),
         VMEM((units, 512, 128), F32),
         VMEM((3, units, 128, 128), F32),
         VMEM((3, units, 32, 128), F32),
-        VMEM((3, units, 8, 128), F32),
-        VMEM((units, 1024, 128), F32),
-    ]
+        VMEM((4, units, 32, 128), F32),
+    ] + [VMEM((units, 1024, 128), F32)] * out
 
 
 S_GROUPS = ((X, 0, 1), (Y, 1, 2), (Z, 3, 1))
@@ -242,32 +257,19 @@
     series_t=((LOOKBACK, ROWS), BF16),
     hid=((ROWS, WIDTH), BF16),
     hid_t=((WIDTH, ROWS), BF16),
-    q_r=((PAIRS, ROWS, 128), F32),
-    q_n=((PAIRS, ROWS, 128), BF16),
-    g_att=((PAIRS, ROWS, 128), BF16),
-    att=((PAIRS, ROWS, 128), BF16),
-    g_query=((PAIRS, ROWS, 128), BF16),
-    g_hid=((ROWS, WIDTH), BF16),
     key_n=((PAIRS, KP, 128), F32),
     key_r=((PAIRS, KP, 128), F32),
     key_in=((PAIRS, 128, 512), BF16),
     key_out=((PAIRS, 512, 128), BF16),
     val_in=((PAIRS, 256, 512), BF16),
     val_out=((PAIRS, 512, 128), BF16),
-    ph_in=((1024, 128), F32),
-    ph_half=((512, 128), F32),
     ph_core=((512, 128), F32),
     ph_plane=((16, 32, 128), F32),
     ph_x=((4, 32, 128), F32),
     ph=((1024, 128), F32),
-    ph_t=((2, WIDTH, KP), BF16),
-    gk=((2, KP, WIDTH), BF16),
-    gv=((2, KP, WIDTH), BF16),
-    back=((2, KP, WIDTH), BF16),
-    out=((ROWS, WIDTH), BF16),
 )
-LOADS = ("w_embed", "proj", "cot", "w_out", "w_query", "w_key", "w_value")
-N_COPIES = 50 + 5 * 3 * 23
+LOADS = ("w_embed", "proj", "w_query", "cot", "w_out", "w_key", "w_value")
+N_COPIES = 50 + 5 * 3 * 20
 
 
 def layer_kernel(*refs):
@@ -276,9 +278,23 @@
     out_hbm, embed_hbm, attn_hbm = refs[8:11]
     refs = refs[11:]
     v = dict(zip(SHAPES, refs[: len(SHAPES)]))
+    for slot, name in enumerate(("att", "g_query", "g_hid", "out")):
+        v[name] = v["series"].at[:, pl.ds(slot * WIDTH, WIDTH)]
+    for slot, name in enumerate(("q_n", "g_att")):
+        v[name] = v["w_embed"].at[pl.ds(slot * ROWS, ROWS)]
     refs = refs[len(SHAPES) :]
-    s_bufs, q0_bufs, q1_bufs, e0_bufs, e1_bufs = (refs[6 * i : 6 * i + 6] for i in range(5))
-    send, recv, load_sem, store_sem = refs[30:]
+    s_bufs, q0_bufs, q1_bufs, e1_bufs = (refs[6 * i : 6 * i + 6] for i in range(4))
+    e0_bufs = refs[24:29] + (s_bufs[0],)
+    send, recv, load_sem, store_sem = refs[29:]
+    v["q_r"] = e1_bufs[0]
+    v["ph_in"] = e0_bufs[0].at[0]
+    v["ph_half"] = e0_bufs[0].at[1, pl.ds(0, 512)]
+    for side in range(2):
+        where = pl.ds(side * KP, KP)
+        v["gk", side] = v["hid_t"].at[where, pl.ds(0, WIDTH)]
+        v["gv", side] = v["hid_t"].at[where, pl.ds(WIDTH, WIDTH)]
+        v["back", side] = v["g_query"].at[where]
+        v["ph_t", side] = v["g_hid"].at[pl.ds(0, WIDTH), pl.ds(side * KP, KP)]
     here = position()
     core, plane = here["c"], here["y"] * 4 + here["z"]
     base = core * 512
@@ -301,8 +317,7 @@
     loads["w_embed"].start()
     for made in series_loads:
         made.start()
-    for name in LOADS[1:]:
-        loads[name].start()
+    loads["proj"].start()
 
     barrier = pltpu.get_barrier_semaphore()
     others = [moved(here, c=1)]
@@ -326,6 +341,9 @@
     loads["w_embed"].wait()
     for block in range(BLOCKS):
         series_loads[block].wait()
+        if block == 2:
+            for name in LOADS[2:]:
+                loads[name].start()
         where = pl.ds(block * BLOCK, BLOCK)
         v["hid"][where] = dot(v["series"][where], v["w_embed"][...]).astype(BF16)
     loads["proj"].wait()
@@ -336,15 +354,17 @@
     pl.semaphore_wait(barrier, len(others))
     across = copies(v["ph_in"].at[rows((1 - core) * 512, 512)], v["ph_core"], moved(here, c=1))
 
-    loads["cot"].wait()
-    loads["w_out"].wait()
+    loads["w_query"].wait()
 
     @pl.loop(0, BLOCKS)
     def _(block):
         where = rows(block * BLOCK, BLOCK)
-        grad = dot_t(v["cot"][where], v["w_out"][...]).astype(BF16)
+        query = dot(v["hid"][where], v["w_query"][...])
         for pair in range(PAIRS):
-            v["g_att"][pair, where] = grad[:, pair * 128 : pair * 128 + 128]
+            part = query[:, pair * 128 : pair * 128 + 128]
+            factor = lax.rsqrt(head_mean(part * part) + 1e-06)
+            v["q_r"][pair, where] = factor
+            v["q_n"][where, pl.ds(pair * 128, 128)] = (part * factor).astype(BF16)
 
     across.wait_recv()
     v["ph_half"][...] = v["ph_in"][rows(base, 512)] + v["ph_core"][...]
@@ -355,19 +375,20 @@
             copies(v["ph_half"].at[rows(there * 32, 32)], v["ph_plane"].at[step], plane_device(step))
         )
 
-    loads["w_query"].wait()
-
-    @pl.loop(0, BLOCKS)
-    def _(block):
-        where = rows(block * BLOCK, BLOCK)
-        query = dot(v["hid"][where], v["w_query"][...])
-        for pair in range(PAIRS):
-            part = query[:, pair * 128 : pair * 128 + 128]
-            factor = lax.rsqrt(head_mean(part * part) + 1e-06)
-            v["q_r"][pair, where] = factor
-            v["q_n"][pair, where] = (part * factor).astype(BF16)
+    @pl.loop(0, 8)
+    def _(part):
+        where = rows(part * 256, 256)
+        v["series_t"][where] = v["series"][:, where].T
 
     own = pl.multiple_of(plane * 32, 32)
+    @pl.loop(0, 8)
+    def _(part):
+        got = dot_t(v["series_t"][rows(part * 256, 256)], v["proj"][...])
+        unit = lax.div(part, 4) * 2
+        where = rows(lax.rem(part, 4) * 256, 256)
+        sum_s.data[unit, where] = got[:, :128]
+        sum_s.data[unit + 1, where] = got[:, 128:]
+
     for made in scattered:
         made.wait_recv()
     total = v["ph_half"][pl.ds(own, 32)]
@@ -376,11 +397,17 @@
     v["ph_x"][here["x"]] = total
     mine = v["ph_x"].at[here["x"]]
     shares = [copies(mine, mine, moved(here, x=step)) for step in (2, 1, 3)]
-
-    @pl.loop(0, 4)
-    def _(part):
-        where = rows(part * 256, 256)
-        v["series_t"][where] = v["series"][:, where].T
+    for group in range(3):
+        sum_s.core(group)
+
+    loads["cot"].wait()
+    loads["w_out"].wait()
+
+    @pl.loop(0, BLOCKS)
+    def _(block):
+        where = rows(block * BLOCK, BLOCK)
+        grad = dot_t(v["cot"][where], v["w_out"][...]).astype(BF16)
+        v["g_att"][where] = grad
 
     for made in shares:
         made.wait_recv()
@@ -389,12 +416,7 @@
     mine[...] = whole
     spread = [copies(mine, mine, plane_device(step)) for step in range(1, 16)]
     passed = [copies(mine, mine, moved(here, c=1))]
-
-    @pl.loop(4, 8)
-    def _(part):
-        where = rows(part * 256, 256)
-        v["series_t"][where] = v["series"][:, where].T
-
+    sum_s.step1()
     v["hid_t"][...] = v["hid"][...].T
 
     for step in range(1, 16):
@@ -403,18 +425,9 @@
         piece = v["ph"].at[rows(base + origin * 32, 32)]
         passed.append(copies(piece, piece, moved(here, c=1)))
 
-    @pl.loop(0, 8)
-    def _(part):
-        got = dot_t(v["series_t"][rows(part * 256, 256)], v["proj"][...])
-        unit = lax.div(part, 4) * 2
-        where = rows(lax.rem(part, 4) * 256, 256)
-        sum_s.data[unit, where] = got[:, :128]
-        sum_s.data[unit + 1, where] = got[:, 128:]
-
     for made in passed:
         made.wait_recv()
-    for group in range(3):
-        sum_s.core(group)
+    copies.drain(16)
 
     loads["w_key"].wait()
     loads["w_value"].wait()
@@ -453,14 +466,15 @@
     def attention(pair):
         sums = sum_q[pair // 2].data
         first = (pair % 2) * 128
+        lanes_of = pl.ds(pair * 128, 128)
         for part in range(4):
             sums[0, pl.ds(part * 256 + first, 128)] = jnp.zeros((128, 128), F32)
 
         @pl.loop(0, BLOCKS)
         def _(block):
             where = rows(block * BLOCK, BLOCK)
-            query = v["q_n"][pair, where]
-            grad = v["g_att"][pair, where]
+            query = v["q_n"][where, lanes_of]
+            grad = v["g_att"][where, lanes_of]
             scores = dot(query, v["key_in"][pair])
             grad_probs = dot(jnp.concatenate([grad, grad], 1), v["val_in"][pair])
             query_t, grad_t = query.T, grad.T
@@ -481,30 +495,28 @@
                         rest = pl.ds(at + side * 256 + first + head * 64, 64)
                         sums[0, rest] = sums[0, rest] + got[:, side * 128 : side * 128 + 128]
             attended = dot(jnp.concatenate(probs_b, 1), v["val_out"][pair])
-            v["att"][pair, where] = attended.astype(BF16)
+            v["att"][where, lanes_of] = attended.astype(BF16)
             grad_n = dot(jnp.concatenate(grad_scores, 1), v["key_out"][pair])
             normed = query.astype(F32)
             grad_q = v["q_r"][pair, where] * (grad_n - normed * head_mean(grad_n * normed))
-            v["g_query"][pair, where] = grad_q.astype(BF16)
+            v["g_query"][where, lanes_of] = grad_q.astype(BF16)
 
     def weight_grads(quad):
-        both = (2 * quad, 2 * quad + 1)
+        both = pl.ds(quad * 256, 256)
         sums = sum_q[quad].data
-        att = jnp.concatenate([v["att"][pair] for pair in both], 1)
-        got = dot(att.T, v["cot"][...])
+        got = dot(v["att"][:, both].T, v["cot"][...])
         for part in range(4):
             sums[2, pl.ds(part * 256, 256)] = got[:, part * 128 : part * 128 + 128]
         sum_q[quad].core(0)
-        got = dot(v["hid_t"][...], jnp.concatenate([v["g_query"][pair] for pair in both], 1))
+        got = dot(v["hid_t"][...], v["g_query"][:, both])
         for part in range(2):
             sums[1, pl.ds(part * 512, 512)] = got[:, part * 128 : part * 128 + 128]
         sum_q[quad].core(1)
         sum_q[quad].core(2)
 
     attention(0)
-    sum_s.step1()
+    sum_s.step2()
     attention(1)
-    sum_s.step2()
     weight_grads(0)
     sum_s.step3()
     attention(2)
@@ -517,14 +529,12 @@
     @pl.loop(0, BLOCKS)
     def _(block):
         where = rows(block * BLOCK, BLOCK)
-        grad = jnp.concatenate([v["g_query"][pair, where] for pair in range(PAIRS)], 1)
         v["g_hid"][where] = (
-            v["cot"][where].astype(F32) + dot_t(grad, v["w_query"][...])
+            v["cot"][where].astype(F32) + dot_t(v["g_query"][where], v["w_query"][...])
         ).astype(BF16)
 
     weight_grads(1)
     sum_q[0].step3()
-    sum_s.step6()
 
     def embed_part(index):
         @pl.loop(0, 4)
@@ -537,23 +547,22 @@
         for group in range(3):
             sum_e[index].core(group)
 
+    sum_s.settle()
     embed_part(0)
     sum_q[1].step1()
     embed_part(1)
     sum_e[0].step1()
     sum_q[0].step4()
-    sum_s.step7()
+    sum_s.step6()
+    sum_e[1].step1()
     sum_q[1].step2()
-    sum_e[1].step1()
-    sum_q[0].step5()
-    sum_q[1].step3()
-    sum_e[0].step2()
 
     @pl.loop(0, BLOCKS)
     def _(block):
         where = rows(block * BLOCK, BLOCK)
-        att = jnp.concatenate([v["att"][pair, where] for pair in range(PAIRS)], 1)
-        v["out"][where] = (v["hid"][where].astype(F32) + dot(att, v["w_out"][...])).astype(BF16)
+        v["out"][where] = (
+            v["hid"][where].astype(F32) + dot(v["att"][where], v["w_out"][...])
+        ).astype(BF16)
 
     stores = []
 
@@ -563,26 +572,25 @@
         stores.append(made)
 
     store(v["out"], out_hbm)
-    sum_q[0].step6()
-    sum_q[1].step4()
+    sum_e[0].step2()
+    sum_q[0].step5()
+    sum_q[1].step3()
     sum_e[1].step2()
     sum_e[0].step3()
-    sum_q[1].step5()
-    sum_q[0].step7()
+    sum_q[1].step4()
+    sum_q[0].step6()
     sum_e[1].step3()
     sum_e[0].step4()
-    sum_q[1].step6()
+    sum_q[1].step5()
     sum_e[1].step4()
     sum_e[0].step5()
-    sum_q[0].all8()
-    sum_s.all8()
-    sum_q[1].step7()
+    sum_q[0].all7()
+    sum_s.all7()
+    for side, part in enumerate(hi_lo(ph)):
+        v["ph_t", side][...] = part.T
+    sum_q[1].step6()
     sum_e[1].step5()
-    sum_e[0].step6()
-    for side, part in enumerate(hi_lo(ph)):
-        v["ph_t"][side] = part.T
-    sum_e[1].step6()
-    sum_q[1].all8()
+    sum_q[1].all7()
     copies.drain()
 
     for quad in range(2):
@@ -605,22 +613,18 @@
             grad_k = v["key_r"][pair] * (grad_n - normed * head_mean(grad_n * normed))
             for index, (name, value) in enumerate((("gk", grad_k), ("gv", turned[1]))):
                 for side, part in enumerate(hi_lo(value)):
-                    v[name][side, :, lanes] = part
-    back = dot_t(v["gk"][0], v["w_key"][...]) + dot_t(v["gk"][1], v["w_key"][...])
-    back = back + dot_t(v["gv"][0], v["w_value"][...]) + dot_t(v["gv"][1], v["w_value"][...])
+                    v[name, side][:, lanes] = part
+    back = dot_t(v["gk", 0][...], v["w_key"][...]) + dot_t(v["gk", 1][...], v["w_key"][...])
+    back = back + dot_t(v["gv", 0][...], v["w_value"][...]) + dot_t(v["gv", 1][...], v["w_value"][...])
     for side, part in enumerate(hi_lo(back)):
-        v["back"][side] = part
+        v["back", side][...] = part
     for index, name in enumerate(("gk", "gv")):
-        got = dot(v["ph_t"][0], v[name][0]) + dot(v["ph_t"][0], v[name][1])
-        got = (got + dot(v["ph_t"][1], v[name][0])) * NORM
+        got = dot(v["ph_t", 0][...], v[name, 0][...]) + dot(v["ph_t", 0][...], v[name, 1][...])
+        got = (got + dot(v["ph_t", 1][...], v[name, 0][...])) * NORM
         for part in range(4):
-            sum_s.data[
-                index * 2 + part // 2, pl.ds((part % 2) * 512, 512)
-            ] = got[:, part * 128 : part * 128 + 128]
-            store(
-                sum_s.data.at[index * 2 + part // 2, pl.ds((part % 2) * 512, 512)],
-                attn_hbm.at[1 + index, :, pl.ds(part * 128, 128)],
-            )
+            where = (part // 2, pl.ds((part % 2) * 512, 512))
+            sum_q[index].data[where] = got[:, part * 128 : part * 128 + 128]
+            store(sum_q[index].data.at[where], attn_hbm.at[1 + index, :, pl.ds(part * 128, 128)])
     for quad in range(2):
         out = sum_q[quad].out
 
@@ -638,8 +642,8 @@
                 out.at[2, pl.ds(part * 256, 256)],
                 attn_hbm.at[3, pl.ds(quad * 256, 256), pl.ds(part * 128, 128)],
             )
-    sum_e[0].step7()
-    sum_e[1].step7()
+    sum_e[0].step6()
+    sum_e[1].step6()
     for index in range(2):
 
         @pl.loop(0, 4)
@@ -647,14 +651,14 @@
             where = rows(part * 256, 256)
             left = jnp.concatenate([sum_s.out[index * 2 + side, where] for side in range(2)], 1)
             left_hi, left_lo = hi_lo(left)
-            got = dot(left_hi, v["back"][0]) + dot(left_hi, v["back"][1])
-            got = got + dot(left_lo, v["back"][0])
+            got = dot(left_hi, v["back", 0][...]) + dot(left_hi, v["back", 1][...])
+            got = got + dot(left_lo, v["back", 0][...])
             for unit in range(4):
                 sum_e[index].data[unit, where] = got[:, unit * 128 : unit * 128 + 128]
 
     for index in range(2):
         for group, (_, start, size) in enumerate(E_GROUPS[index]):
-            sum_e[index].step8(group)
+            sum_e[index].step7(group)
             if group == 2:
                 copies.drain()
         for unit in range(4):
@@ -689,7 +693,8 @@
         scratch_shapes=[VMEM(shape, dtype) for shape, dtype in SHAPES.values()]
         + sum_bufs(4)
         + sum_bufs(3) * 2
-        + sum_bufs(4) * 2
+        + sum_bufs(4)
+        + sum_bufs(4, False)
         + [
             pltpu.SemaphoreType.DMA((N_COPIES,)),
             pltpu.SemaphoreType.DMA((N_COPIES,)),

time: 126 us -> 115 us (0.913)
  Pallas kernels: 115 us -> 105 us
    pallas_call x1, Pallas kernels: 115 us -> 105 us  [local(): pl.pallas_call(layer_kernel, out_shape=(jax.ShapeDtypeStruct((ROWS, WIDTH...]
where the time goes in v3:
time: 115 us
  Pallas kernels  105 us (91%)
  local copies, waits for them, and re-layouts  9.1 us (8%)
    pallas_call x1, Pallas kernels, local(): pl.pallas_call(layer_kernel, out_shape=(jax.ShapeDtypeStruct((ROWS, WIDTH...  105 us
    unnamed x5, local copies, waits for them, and re-layouts  9.1 us

profile of v3, /device:TPU:1, one launch (start us, length us, event | category | flops | bytes accessed | tf_op | source)
XLA Modules:
  0.0 114.7 jit_solution(10661065071511668098)
XLA Ops:
  0.6 105.0 %shard_map.103 = (bf16[1024,512]{1,0:T(8,128)(2,1)}, f32[2048,512]{1,0:T(8,128)}, f32[4,512,512]{2,1,0:T(8,128)}) custom-call(bf16[1024,2048]{1,0:T(8,128)(2,1)} %refs_0_.1, bf16[2048,512]{1,0:T(8,128)(2,1)} %refs_1_.1, bf16[512,512]{1,0:T(8,128)(2,1)} %refs_2_.1, bf16[512,512]{1,0:T(8,128)(2,1)} %refs_3_.1, bf16[512,512]{1,0:T(8,128)(2,1)} %refs_4_.1, ...), custom_call_target="tpu_custom_call" | custom-call | tf_op jit(solution)/shard_map/pallas_call | solution.py:684
  105.6 2.3 %copy.14 = bf16[1024,512]{1,0:T(8,128)(2,1)} copy(bf16[1024,512]{1,0:T(8,128)(2,1)} %get-tuple-element.6) | data formatting | bytes 2097152
  107.9 0.0 copy-start
  107.9 4.8 %copy.15 = f32[2048,512]{1,0:T(8,128)} copy(f32[2048,512]{1,0:T(8,128)} %get-tuple-element.7) | data formatting | bytes 8388608
  112.7 0.0 copy-done
  112.7 2.0 %copy.16 = f32[4,512,512]{2,1,0:T(8,128)} copy(f32[4,512,512]{2,1,0:T(8,128)S(1)} %copy-done) | data formatting | bytes 8388608
Async XLA Ops:
  107.9 4.8 %copy-start = (f32[4,512,512]{2,1,0:T(8,128)S(1)}, f32[4,512,512]{2,1,0:T(8,128)}, u32[]{:S(2)}) copy-start(f32[4,512,512]{2,1,0:T(8,128)} %get-tuple-element.8) | copy-start | bytes 12582916

commit v4 on v3

--- a/solution.py
+++ b/solution.py
@@ -56,99 +56,115 @@
     return (there["x"] * 8 + there["y"] * 2 + there["c"], there["z"])
 
 
-class Copies:
-    def __init__(self, send, recv):
-        self.send, self.recv = send, recv
-        self.count = 0
-        self.waiting = []
-
-    def __call__(self, src, dst, device):
-        slot = self.count
-        self.count += 1
-        made = pltpu.make_async_remote_copy(
+class Batch:
+    def __init__(self, pool, whole):
+        slot = pool.count
+        pool.count += 1
+        pool.open.append(self)
+        self.send, self.recv, self.whole = pool.send.at[slot], pool.recv.at[slot], whole
+
+    def add(self, src, dst, device):
+        self.device = device
+        self.copy(src, dst).start()
+
+    def copy(self, src, dst):
+        return pltpu.make_async_remote_copy(
             src_ref=src,
             dst_ref=dst,
-            send_sem=self.send.at[slot],
-            recv_sem=self.recv.at[slot],
-            device_id=device,
+            send_sem=self.send,
+            recv_sem=self.recv,
+            device_id=self.device,
             device_id_type=MESH,
         )
-        made.start()
-        self.waiting.append(made)
-        return made
-
-    def drain(self, first=None):
-        for made in self.waiting[:first]:
-            made.wait_send()
-        self.waiting = self.waiting[len(self.waiting) if first is None else first :]
+
+    def wait_recv(self):
+        self.copy(self.whole, self.whole).wait_recv()
+
+    def wait_send(self):
+        self.copy(self.whole, self.whole).wait_send()
+
+
+class Pool:
+    def __init__(self, send, recv):
+        self.send, self.recv, self.count, self.open = send, recv, 0, []
+
+    def batch(self, whole):
+        return Batch(self, whole)
+
+    def drain(self, batches=None):
+        for one in list(self.open) if batches is None else batches:
+            one.wait_send()
+            self.open.remove(one)
 
 
 X, Y, Z = ("x", "y", "z"), ("y", "z", "x"), ("z", "x", "y")
 
 
 class Sum:
-    def __init__(self, here, copies, groups, bufs):
-        self.here, self.copy, self.groups = here, copies, groups
+    def __init__(self, here, pool, groups, bufs):
+        self.here, self.pool, self.groups = here, pool, groups
         self.data, self.half, self.one, self.two, self.three, self.out = bufs
         self.base = here["c"] * 512
         self.across = []
         self.made = {}
+        self.passed = []
         self.sends = []
+        self.batches = []
+
+    def batch(self, whole):
+        self.batches.append(self.pool.batch(whole))
+        return self.batches[-1]
+
+    def finish(self):
+        self.pool.drain([one for one in self.batches if one in self.pool.open])
+
+    def units(self, group):
+        return pl.ds(self.groups[group][1], self.groups[group][2])
 
     def core(self, group):
-        _, start, size = self.groups[group]
-        units = pl.ds(start, size)
-        self.across.append(
-            self.copy(
-                self.data.at[units, rows((1 - self.here["c"]) * 512, 512)],
-                self.half.at[units],
-                moved(self.here, c=1),
-            )
+        units = self.units(group)
+        self.across.append(self.batch(self.half.at[units]))
+        self.sends.append(self.across[-1])
+        self.across[-1].add(
+            self.data.at[units, rows((1 - self.here["c"]) * 512, 512)],
+            self.half.at[units],
+            moved(self.here, c=1),
         )
-        self.sends.append(self.across[-1])
 
     def place(self, group, level):
-        order = self.groups[group][0]
-        sizes = (128, 32)
         at = self.base
-        for axis, size in zip(order[:level], sizes[:level]):
+        for axis, size in zip(self.groups[group][0][:level], (128, 32)):
             at = at + self.here[axis] * size
         return at
 
     def scatter(self, level, group):
-        order, start, size = self.groups[group]
-        axis = order[level]
+        units = self.units(group)
+        axis = self.groups[group][0][level]
         extent = (128, 32)[level]
         buffer = (self.one, self.two)[level]
         at = self.place(group, level)
-        self.made[group] = [
-            self.copy(
+        self.made[group] = self.batch(buffer.at[:, units])
+        self.sends.append(self.made[group])
+        for step in (2, 1, 3):
+            self.made[group].add(
                 self.data.at[
-                    pl.ds(start, size),
-                    rows(at + lax.rem(self.here[axis] + step, 4) * extent, extent),
+                    units, rows(at + lax.rem(self.here[axis] + step, 4) * extent, extent)
                 ],
-                buffer.at[step - 1, pl.ds(start, size)],
+                buffer.at[step - 1, units],
                 moved(self.here, **{axis: step}),
             )
-            for step in (2, 1, 3)
-        ]
-        self.sends += self.made[group]
 
     def settle(self):
-        for made in self.sends:
-            made.wait_send()
-        self.copy.waiting = [
-            made for made in self.copy.waiting if not any(made is one for one in self.sends)
-        ]
+        self.pool.drain(self.sends)
 
     def gather(self, level, group):
-        order, start, size = self.groups[group]
-        axis = order[level]
+        units = self.units(group)
+        axis = self.groups[group][0][level]
         extent = (128, 32)[level]
-        own = self.out.at[pl.ds(start, size), rows(self.place(group, level + 1), extent)]
-        self.made[group] = [
-            self.copy(own, own, moved(self.here, **{axis: step})) for step in (2, 1, 3)
-        ]
+        own = self.out.at[units, rows(self.place(group, level + 1), extent)]
+        self.made[group] = self.batch(self.out.at[units, pl.ds(0, 3 * extent)])
+        for step in (2, 1, 3):
+            self.made[group].add(own, own, moved(self.here, **{axis: step}))
         return own
 
     def step1(self):
@@ -163,12 +179,11 @@
             self.scatter(0, group)
 
     def reduced(self, level, group):
-        order, start, size = self.groups[group]
+        order = self.groups[group][0]
         extent = (128, 32)[level]
         buffer = (self.one, self.two)[level]
-        for made in self.made[group]:
-            made.wait_recv()
-        units = pl.ds(start, size)
+        self.made[group].wait_recv()
+        units = self.units(group)
         where = (units, rows(self.place(group, level + 1), extent))
         total = (self.data[where] + buffer[0, units]) + (buffer[1, units] + buffer[2, units])
         if level == 0:
@@ -176,14 +191,13 @@
         else:
             mine = (self.here[order[2]], units)
             self.three[mine] = total
-            self.made[group] = [
-                self.copy(
+            self.made[group] = self.batch(self.three.at[pl.ds(0, 3), units])
+            for step in (2, 1, 3):
+                self.made[group].add(
                     self.three.at[mine],
                     self.three.at[mine],
                     moved(self.here, **{order[2]: step}),
                 )
-                for step in (2, 1, 3)
-            ]
 
     def step2(self):
         for group in range(len(self.groups)):
@@ -195,36 +209,33 @@
             self.reduced(1, group)
 
     def step4(self):
-        for group, (_, start, size) in enumerate(self.groups):
-            self.gathered(group)
-            units = pl.ds(start, size)
+        for group in range(len(self.groups)):
+            self.made[group].wait_recv()
+            units = self.units(group)
             part = [self.three[index, units] for index in range(4)]
             where = (units, rows(self.place(group, 2), 32))
             self.out[where] = (part[0] + part[1]) + (part[2] + part[3])
             self.gather(1, group)
 
-    def gathered(self, group):
-        for made in self.made[group]:
-            made.wait_recv()
-
     def step5(self):
-        self.passed = []
         for group in range(len(self.groups)):
-            self.gathered(group)
+            self.made[group].wait_recv()
             own = self.gather(0, group)
-            self.passed.append([self.copy(own, own, moved(self.here, c=1))])
+            self.passed.append(
+                self.batch(self.out.at[self.units(group), pl.ds(0, 512)])
+            )
+            self.passed[group].add(own, own, moved(self.here, c=1))
 
     def step6(self):
-        for group, (order, start, size) in enumerate(self.groups):
-            for made, step in zip(self.made[group], (2, 1, 3)):
-                made.wait_recv()
+        for group, (order, _, _) in enumerate(self.groups):
+            self.made[group].wait_recv()
+            for step in (2, 1, 3):
                 chunk = lax.rem(self.here[order[0]] + 4 - step, 4)
-                piece = self.out.at[pl.ds(start, size), rows(self.base + chunk * 128, 128)]
-                self.passed[group].append(self.copy(piece, piece, moved(self.here, c=1)))
+                piece = self.out.at[self.units(group), rows(self.base + chunk * 128, 128)]
+                self.passed[group].add(piece, piece, moved(self.here, c=1))
 
     def step7(self, group):
-        for made in self.passed[group]:
-            made.wait_recv()
+        self.passed[group].wait_recv()
 
     def all7(self):
         for group in range(len(self.groups)):
@@ -263,13 +274,16 @@
     key_out=((PAIRS, 512, 128), BF16),
     val_in=((PAIRS, 256, 512), BF16),
     val_out=((PAIRS, 512, 128), BF16),
+    proj_t=((ROWS, KP), BF16),
+    w_out_t=((WIDTH, WIDTH), BF16),
+    w_query_t=((WIDTH, WIDTH), BF16),
     ph_core=((512, 128), F32),
-    ph_plane=((16, 32, 128), F32),
+    ph_plane=((15, 32, 128), F32),
     ph_x=((4, 32, 128), F32),
     ph=((1024, 128), F32),
 )
 LOADS = ("w_embed", "proj", "w_query", "cot", "w_out", "w_key", "w_value")
-N_COPIES = 50 + 5 * 3 * 20
+N_COPIES = 5 + 5 * 3 * 7
 
 
 def layer_kernel(*refs):
@@ -326,10 +340,10 @@
     for device in others:
         pl.semaphore_signal(barrier, inc=1, device_id=device, device_id_type=MESH)
 
-    copies = Copies(send, recv)
-    sum_s = Sum(here, copies, S_GROUPS, s_bufs)
-    sum_q = [Sum(here, copies, Q_GROUPS, bufs) for bufs in (q0_bufs, q1_bufs)]
-    sum_e = [Sum(here, copies, E_GROUPS[i], bufs) for i, bufs in enumerate((e0_bufs, e1_bufs))]
+    pool = Pool(send, recv)
+    sum_s = Sum(here, pool, S_GROUPS, s_bufs)
+    sum_q = [Sum(here, pool, Q_GROUPS, bufs) for bufs in (q0_bufs, q1_bufs)]
+    sum_e = [Sum(here, pool, E_GROUPS[i], bufs) for i, bufs in enumerate((e0_bufs, e1_bufs))]
 
     lane = lax.broadcasted_iota(jnp.int32, (256, 128), 1) & 64
     row = lax.broadcasted_iota(jnp.int32, (256, 128), 0) & 64
@@ -352,7 +366,8 @@
         v["ph_in"][pl.ds(pair * 256, 256)] = part[:, pair * 128 : pair * 128 + 128]
 
     pl.semaphore_wait(barrier, len(others))
-    across = copies(v["ph_in"].at[rows((1 - core) * 512, 512)], v["ph_core"], moved(here, c=1))
+    across = pool.batch(v["ph_core"])
+    across.add(v["ph_in"].at[rows((1 - core) * 512, 512)], v["ph_core"], moved(here, c=1))
 
     loads["w_query"].wait()
 
@@ -368,11 +383,11 @@
 
     across.wait_recv()
     v["ph_half"][...] = v["ph_in"][rows(base, 512)] + v["ph_core"][...]
-    scattered = []
+    scattered = pool.batch(v["ph_plane"])
     for step in range(1, 16):
         there = lax.rem(plane + step, 16)
-        scattered.append(
-            copies(v["ph_half"].at[rows(there * 32, 32)], v["ph_plane"].at[step], plane_device(step))
+        scattered.add(
+            v["ph_half"].at[rows(there * 32, 32)], v["ph_plane"].at[step - 1], plane_device(step)
         )
 
     @pl.loop(0, 8)
@@ -381,53 +396,54 @@
         v["series_t"][where] = v["series"][:, where].T
 
     own = pl.multiple_of(plane * 32, 32)
+    v["proj_t"][...] = v["proj"][...].T
     @pl.loop(0, 8)
     def _(part):
-        got = dot_t(v["series_t"][rows(part * 256, 256)], v["proj"][...])
+        got = dot(v["series_t"][rows(part * 256, 256)], v["proj_t"][...])
         unit = lax.div(part, 4) * 2
         where = rows(lax.rem(part, 4) * 256, 256)
         sum_s.data[unit, where] = got[:, :128]
         sum_s.data[unit + 1, where] = got[:, 128:]
 
-    for made in scattered:
-        made.wait_recv()
+    scattered.wait_recv()
     total = v["ph_half"][pl.ds(own, 32)]
-    for step in range(1, 16):
+    for step in range(15):
         total = total + v["ph_plane"][step]
     v["ph_x"][here["x"]] = total
     mine = v["ph_x"].at[here["x"]]
-    shares = [copies(mine, mine, moved(here, x=step)) for step in (2, 1, 3)]
+    shares = pool.batch(v["ph_x"].at[pl.ds(0, 3)])
+    for step in (2, 1, 3):
+        shares.add(mine, mine, moved(here, x=step))
     for group in range(3):
         sum_s.core(group)
 
     loads["cot"].wait()
     loads["w_out"].wait()
+    v["w_out_t"][...] = v["w_out"][...].T
+    v["w_query_t"][...] = v["w_query"][...].T
 
     @pl.loop(0, BLOCKS)
     def _(block):
         where = rows(block * BLOCK, BLOCK)
-        grad = dot_t(v["cot"][where], v["w_out"][...]).astype(BF16)
+        grad = dot(v["cot"][where], v["w_out_t"][...]).astype(BF16)
         v["g_att"][where] = grad
 
-    for made in shares:
-        made.wait_recv()
+    shares.wait_recv()
     whole = (v["ph_x"][0] + v["ph_x"][1]) + (v["ph_x"][2] + v["ph_x"][3])
     mine = v["ph"].at[rows(base + own, 32)]
     mine[...] = whole
-    spread = [copies(mine, mine, plane_device(step)) for step in range(1, 16)]
-    passed = [copies(mine, mine, moved(here, c=1))]
+    spread = pool.batch(v["ph"].at[pl.ds(0, 480)])
+    for step in range(1, 16):
+        spread.add(mine, mine, plane_device(step))
     sum_s.step1()
     v["hid_t"][...] = v["hid"][...].T
 
-    for step in range(1, 16):
-        spread[step - 1].wait_recv()
-        origin = lax.rem(plane + 16 - step, 16)
-        piece = v["ph"].at[rows(base + origin * 32, 32)]
-        passed.append(copies(piece, piece, moved(here, c=1)))
-
-    for made in passed:
-        made.wait_recv()
-    copies.drain(16)
+    spread.wait_recv()
+    mine = v["ph"].at[rows(base, 512)]
+    passed = pool.batch(mine)
+    passed.add(mine, mine, moved(here, c=1))
+    passed.wait_recv()
+    pool.drain([across, scattered])
 
     loads["w_key"].wait()
     loads["w_value"].wait()
@@ -530,7 +546,7 @@
     def _(block):
         where = rows(block * BLOCK, BLOCK)
         v["g_hid"][where] = (
-            v["cot"][where].astype(F32) + dot_t(v["g_query"][where], v["w_query"][...])
+            v["cot"][where].astype(F32) + dot(v["g_query"][where], v["w_query_t"][...])
         ).astype(BF16)
 
     weight_grads(1)
@@ -591,7 +607,10 @@
     sum_q[1].step6()
     sum_e[1].step5()
     sum_q[1].all7()
-    copies.drain()
+    for one in sum_e:
+        one.settle()
+    for one in sum_q:
+        one.finish()
 
     for quad in range(2):
         for half in range(2):
@@ -659,8 +678,7 @@
     for index in range(2):
         for group, (_, start, size) in enumerate(E_GROUPS[index]):
             sum_e[index].step7(group)
-            if group == 2:
-                copies.drain()
+        sum_e[index].finish()
         for unit in range(4):
 
             @pl.loop(0, 4)
@@ -674,7 +692,7 @@
                 sum_e[index].out.at[unit],
                 embed_hbm.at[pl.ds(index * 1024, 1024), pl.ds(unit * 128, 128)],
             )
-    copies.drain()
+    pool.drain()
     for made in stores:
         made.wait()
 

time: 115 us -> 110 us (0.957)
  Pallas kernels: 105 us -> 100 us
    pallas_call x1, Pallas kernels: 105 us -> 100 us  [local(): pl.pallas_call(layer_kernel, out_shape=(jax.ShapeDtypeStruct((ROWS, WIDTH...]
where the time goes in v4:
time: 110 us
  Pallas kernels  100 us (91%)
  local copies, waits for them, and re-layouts  9.1 us (8%)
    pallas_call x1, Pallas kernels, local(): pl.pallas_call(layer_kernel, out_shape=(jax.ShapeDtypeStruct((ROWS, WIDTH...  100 us
    unnamed x5, local copies, waits for them, and re-layouts  9.1 us

profile of v4, /device:TPU:1, one launch (start us, length us, event | category | flops | bytes accessed | tf_op | source)
XLA Modules:
  0.0 109.8 jit_solution(8073274108724211491)
XLA Ops:
  0.6 100.1 %shard_map.103 = (bf16[1024,512]{1,0:T(8,128)(2,1)}, f32[2048,512]{1,0:T(8,128)}, f32[4,512,512]{2,1,0:T(8,128)}) custom-call(bf16[1024,2048]{1,0:T(8,128)(2,1)} %refs_0_.1, bf16[2048,512]{1,0:T(8,128)(2,1)} %refs_1_.1, bf16[512,512]{1,0:T(8,128)(2,1)} %refs_2_.1, bf16[512,512]{1,0:T(8,128)(2,1)} %refs_3_.1, bf16[512,512]{1,0:T(8,128)(2,1)} %refs_4_.1, ...), custom_call_target="tpu_custom_call" | custom-call | tf_op jit(solution)/shard_map/pallas_call | solution.py:702
  100.7 2.3 %copy.14 = bf16[1024,512]{1,0:T(8,128)(2,1)} copy(bf16[1024,512]{1,0:T(8,128)(2,1)} %get-tuple-element.6) | data formatting | bytes 2097152
  103.0 0.0 copy-start
  103.0 4.8 %copy.15 = f32[2048,512]{1,0:T(8,128)} copy(f32[2048,512]{1,0:T(8,128)} %get-tuple-element.7) | data formatting | bytes 8388608
  107.8 0.0 copy-done
  107.8 2.0 %copy.16 = f32[4,512,512]{2,1,0:T(8,128)} copy(f32[4,512,512]{2,1,0:T(8,128)S(1)} %copy-done) | data formatting | bytes 8388608
Async XLA Ops:
  103.0 4.8 %copy-start = (f32[4,512,512]{2,1,0:T(8,128)S(1)}, f32[4,512,512]{2,1,0:T(8,128)}, u32[]{:S(2)}) copy-start(f32[4,512,512]{2,1,0:T(8,128)} %get-tuple-element.8) | copy-start | bytes 12582916

commit v5 on v4

--- a/solution.py
+++ b/solution.py
@@ -17,7 +17,8 @@
 LOOKBACK = 2048
 KP = 256
 PAIRS = 4
-BLOCK = 256
+BLOCK = 512
+LOADS_OF_SERIES = 4
 BLOCKS = ROWS // BLOCK
 NORM = 1.0 / math.sqrt(131072.0)
 
@@ -321,8 +322,8 @@
     for slot, name in enumerate(LOADS):
         loads[name] = pltpu.make_async_copy(hbm[name], v[name], load_sem.at[slot])
     series_loads = []
-    for block in range(BLOCKS):
-        where = pl.ds(block * BLOCK, BLOCK)
+    for block in range(LOADS_OF_SERIES):
+        where = pl.ds(block * 256, 256)
         series_loads.append(
             pltpu.make_async_copy(
                 hbm["series"].at[where], v["series"].at[where], load_sem.at[len(LOADS) + block]
@@ -354,8 +355,9 @@
 
     loads["w_embed"].wait()
     for block in range(BLOCKS):
-        series_loads[block].wait()
-        if block == 2:
+        series_loads[2 * block].wait()
+        series_loads[2 * block + 1].wait()
+        if block == 1:
             for name in LOADS[2:]:
                 loads[name].start()
         where = pl.ds(block * BLOCK, BLOCK)
@@ -397,11 +399,11 @@
 
     own = pl.multiple_of(plane * 32, 32)
     v["proj_t"][...] = v["proj"][...].T
-    @pl.loop(0, 8)
+    @pl.loop(0, 4)
     def _(part):
-        got = dot(v["series_t"][rows(part * 256, 256)], v["proj_t"][...])
-        unit = lax.div(part, 4) * 2
-        where = rows(lax.rem(part, 4) * 256, 256)
+        got = dot(v["series_t"][rows(part * 512, 512)], v["proj_t"][...])
+        unit = lax.div(part, 2) * 2
+        where = rows(lax.rem(part, 2) * 512, 512)
         sum_s.data[unit, where] = got[:, :128]
         sum_s.data[unit + 1, where] = got[:, 128:]
 
@@ -444,6 +446,7 @@
     passed.add(mine, mine, moved(here, c=1))
     passed.wait_recv()
     pool.drain([across, scattered])
+    sum_s.step2()
 
     loads["w_key"].wait()
     loads["w_value"].wait()
@@ -531,16 +534,13 @@
         sum_q[quad].core(2)
 
     attention(0)
-    sum_s.step2()
     attention(1)
     weight_grads(0)
     sum_s.step3()
     attention(2)
+    attention(3)
     sum_q[0].step1()
     sum_s.step4()
-    attention(3)
-    sum_q[0].step2()
-    sum_s.step5()
 
     @pl.loop(0, BLOCKS)
     def _(block):
@@ -550,13 +550,12 @@
         ).astype(BF16)
 
     weight_grads(1)
-    sum_q[0].step3()
 
     def embed_part(index):
-        @pl.loop(0, 4)
+        @pl.loop(0, 2)
         def _(part):
-            got = dot(v["series_t"][rows(index * 1024 + part * 256, 256)], v["g_hid"][...])
-            where = rows(part * 256, 256)
+            got = dot(v["series_t"][rows(index * 1024 + part * 512, 512)], v["g_hid"][...])
+            where = rows(part * 512, 512)
             for unit in range(4):
                 sum_e[index].data[unit, where] = got[:, unit * 128 : unit * 128 + 128]
 
@@ -566,12 +565,13 @@
     sum_s.settle()
     embed_part(0)
     sum_q[1].step1()
+    sum_q[0].step2()
     embed_part(1)
     sum_e[0].step1()
-    sum_q[0].step4()
-    sum_s.step6()
+    sum_s.step5()
     sum_e[1].step1()
     sum_q[1].step2()
+    sum_q[0].step3()
 
     @pl.loop(0, BLOCKS)
     def _(block):
@@ -589,19 +589,21 @@
 
     store(v["out"], out_hbm)
     sum_e[0].step2()
-    sum_q[0].step5()
     sum_q[1].step3()
+    sum_q[0].step4()
     sum_e[1].step2()
     sum_e[0].step3()
     sum_q[1].step4()
-    sum_q[0].step6()
+    sum_s.step6()
+    sum_q[0].step5()
     sum_e[1].step3()
     sum_e[0].step4()
     sum_q[1].step5()
     sum_e[1].step4()
     sum_e[0].step5()
+    sum_q[0].step6()
+    sum_s.all7()
     sum_q[0].all7()
-    sum_s.all7()
     for side, part in enumerate(hi_lo(ph)):
         v["ph_t", side][...] = part.T
     sum_q[1].step6()
@@ -716,7 +718,7 @@
         + [
             pltpu.SemaphoreType.DMA((N_COPIES,)),
             pltpu.SemaphoreType.DMA((N_COPIES,)),
-            pltpu.SemaphoreType.DMA((len(LOADS) + BLOCKS,)),
+            pltpu.SemaphoreType.DMA((len(LOADS) + LOADS_OF_SERIES,)),
             pltpu.SemaphoreType.DMA((32,)),
         ],
         compiler_params=pltpu.CompilerParams(

time: 110 us -> 105 us (0.955)
  Pallas kernels: 100 us -> 95.6 us
    pallas_call x1, Pallas kernels: 100 us -> 95.6 us  [local(): pl.pallas_call(layer_kernel, out_shape=(jax.ShapeDtypeStruct((ROWS, WIDTH...]
where the time goes in v5:
time: 105 us
  Pallas kernels  95.6 us (91%)
  local copies, waits for them, and re-layouts  9.1 us (9%)
    pallas_call x1, Pallas kernels, local(): pl.pallas_call(layer_kernel, out_shape=(jax.ShapeDtypeStruct((ROWS, WIDTH...  95.6 us
    unnamed x5, local copies, waits for them, and re-layouts  9.1 us

profile of v5, /device:TPU:1, one launch (start us, length us, event | category | flops | bytes accessed | tf_op | source)
XLA Modules:
  0.0 105.3 jit_solution(550490797336969514)
XLA Ops:
  0.6 95.6 %shard_map.103 = (bf16[1024,512]{1,0:T(8,128)(2,1)}, f32[2048,512]{1,0:T(8,128)}, f32[4,512,512]{2,1,0:T(8,128)}) custom-call(bf16[1024,2048]{1,0:T(8,128)(2,1)} %refs_0_.1, bf16[2048,512]{1,0:T(8,128)(2,1)} %refs_1_.1, bf16[512,512]{1,0:T(8,128)(2,1)} %refs_2_.1, bf16[512,512]{1,0:T(8,128)(2,1)} %refs_3_.1, bf16[512,512]{1,0:T(8,128)(2,1)} %refs_4_.1, ...), custom_call_target="tpu_custom_call" | custom-call | tf_op jit(solution)/shard_map/pallas_call | solution.py:704
  96.2 2.3 %copy.14 = bf16[1024,512]{1,0:T(8,128)(2,1)} copy(bf16[1024,512]{1,0:T(8,128)(2,1)} %get-tuple-element.6) | data formatting | bytes 2097152
  98.5 0.0 copy-start
  98.5 4.8 %copy.15 = f32[2048,512]{1,0:T(8,128)} copy(f32[2048,512]{1,0:T(8,128)} %get-tuple-element.7) | data formatting | bytes 8388608
  103.3 0.0 copy-done
  103.3 2.0 %copy.16 = f32[4,512,512]{2,1,0:T(8,128)} copy(f32[4,512,512]{2,1,0:T(8,128)S(1)} %copy-done) | data formatting | bytes 8388608
Async XLA Ops:
  98.5 4.8 %copy-start = (f32[4,512,512]{2,1,0:T(8,128)S(1)}, f32[4,512,512]{2,1,0:T(8,128)}, u32[]{:S(2)}) copy-start(f32[4,512,512]{2,1,0:T(8,128)} %get-tuple-element.8) | copy-start | bytes 12582916

commit v6 on v5

--- a/solution.py
+++ b/solution.py
@@ -18,6 +18,7 @@
 KP = 256
 PAIRS = 4
 BLOCK = 512
+ATTENTION_BLOCK = 512
 LOADS_OF_SERIES = 4
 BLOCKS = ROWS // BLOCK
 NORM = 1.0 / math.sqrt(131072.0)
@@ -63,6 +64,7 @@
         pool.count += 1
         pool.open.append(self)
         self.send, self.recv, self.whole = pool.send.at[slot], pool.recv.at[slot], whole
+        self.arrived = False
 
     def add(self, src, dst, device):
         self.device = device
@@ -79,7 +81,9 @@
         )
 
     def wait_recv(self):
-        self.copy(self.whole, self.whole).wait_recv()
+        if not self.arrived:
+            self.copy(self.whole, self.whole).wait_recv()
+        self.arrived = True
 
     def wait_send(self):
         self.copy(self.whole, self.whole).wait_send()
@@ -102,7 +106,8 @@
 
 
 class Sum:
-    def __init__(self, here, pool, groups, bufs):
+    def __init__(self, here, pool, groups, bufs, joined=False):
+        self.joined = joined
         self.here, self.pool, self.groups = here, pool, groups
         self.data, self.half, self.one, self.two, self.three, self.out = bufs
         self.base = here["c"] * 512
@@ -112,9 +117,14 @@
         self.sends = []
         self.batches = []
 
-    def batch(self, whole):
-        self.batches.append(self.pool.batch(whole))
+    def batch(self, group, whole, first):
+        if self.joined and group > 0:
+            return first
+        self.batches.append(self.pool.batch(whole(self.waits(group))))
         return self.batches[-1]
+
+    def waits(self, group):
+        return slice(None) if self.joined else self.units(group)
 
     def finish(self):
         self.pool.drain([one for one in self.batches if one in self.pool.open])
@@ -124,7 +134,8 @@
 
     def core(self, group):
         units = self.units(group)
-        self.across.append(self.batch(self.half.at[units]))
+        first = self.across[0] if self.across else None
+        self.across.append(self.batch(group, lambda some: self.half.at[some], first))
         self.sends.append(self.across[-1])
         self.across[-1].add(
             self.data.at[units, rows((1 - self.here["c"]) * 512, 512)],
@@ -144,7 +155,7 @@
         extent = (128, 32)[level]
         buffer = (self.one, self.two)[level]
         at = self.place(group, level)
-        self.made[group] = self.batch(buffer.at[:, units])
+        self.made[group] = self.batch(group, lambda some: buffer.at[:, some], self.made.get(0))
         self.sends.append(self.made[group])
         for step in (2, 1, 3):
             self.made[group].add(
@@ -156,14 +167,16 @@
             )
 
     def settle(self):
-        self.pool.drain(self.sends)
+        self.pool.drain([one for one in self.batches if one in self.sends])
 
     def gather(self, level, group):
         units = self.units(group)
         axis = self.groups[group][0][level]
         extent = (128, 32)[level]
         own = self.out.at[units, rows(self.place(group, level + 1), extent)]
-        self.made[group] = self.batch(self.out.at[units, pl.ds(0, 3 * extent)])
+        self.made[group] = self.batch(
+            group, lambda some: self.out.at[some, pl.ds(0, 3 * extent)], self.made.get(0)
+        )
         for step in (2, 1, 3):
             self.made[group].add(own, own, moved(self.here, **{axis: step}))
         return own
@@ -192,7 +205,9 @@
         else:
             mine = (self.here[order[2]], units)
             self.three[mine] = total
-            self.made[group] = self.batch(self.three.at[pl.ds(0, 3), units])
+            self.made[group] = self.batch(
+                group, lambda some: self.three.at[pl.ds(0, 3), some], self.made.get(0)
+            )
             for step in (2, 1, 3):
                 self.made[group].add(
                     self.three.at[mine],
@@ -222,8 +237,9 @@
         for group in range(len(self.groups)):
             self.made[group].wait_recv()
             own = self.gather(0, group)
+            first = self.passed[0] if self.passed else None
             self.passed.append(
-                self.batch(self.out.at[self.units(group), pl.ds(0, 512)])
+                self.batch(group, lambda some: self.out.at[some, pl.ds(0, 512)], first)
             )
             self.passed[group].add(own, own, moved(self.here, c=1))
 
@@ -284,7 +300,7 @@
     ph=((1024, 128), F32),
 )
 LOADS = ("w_embed", "proj", "w_query", "cot", "w_out", "w_key", "w_value")
-N_COPIES = 5 + 5 * 3 * 7
+N_COPIES = 5 + 3 * 7 + 2 * 3 * 7
 
 
 def layer_kernel(*refs):
@@ -342,8 +358,8 @@
         pl.semaphore_signal(barrier, inc=1, device_id=device, device_id_type=MESH)
 
     pool = Pool(send, recv)
-    sum_s = Sum(here, pool, S_GROUPS, s_bufs)
-    sum_q = [Sum(here, pool, Q_GROUPS, bufs) for bufs in (q0_bufs, q1_bufs)]
+    sum_s = Sum(here, pool, S_GROUPS, s_bufs, True)
+    sum_q = [Sum(here, pool, Q_GROUPS, bufs, True) for bufs in (q0_bufs, q1_bufs)]
     sum_e = [Sum(here, pool, E_GROUPS[i], bufs) for i, bufs in enumerate((e0_bufs, e1_bufs))]
 
     lane = lax.broadcasted_iota(jnp.int32, (256, 128), 1) & 64
@@ -371,6 +387,20 @@
     across = pool.batch(v["ph_core"])
     across.add(v["ph_in"].at[rows((1 - core) * 512, 512)], v["ph_core"], moved(here, c=1))
 
+    across.wait_recv()
+    v["ph_half"][...] = v["ph_in"][rows(base, 512)] + v["ph_core"][...]
+    scattered = pool.batch(v["ph_plane"])
+    for step in range(1, 16):
+        there = lax.rem(plane + step, 16)
+        scattered.add(
+            v["ph_half"].at[rows(there * 32, 32)], v["ph_plane"].at[step - 1], plane_device(step)
+        )
+
+    @pl.loop(0, 8)
+    def _(part):
+        where = rows(part * 256, 256)
+        v["series_t"][where] = v["series"][:, where].T
+
     loads["w_query"].wait()
 
     @pl.loop(0, BLOCKS)
@@ -382,20 +412,6 @@
             factor = lax.rsqrt(head_mean(part * part) + 1e-06)
             v["q_r"][pair, where] = factor
             v["q_n"][where, pl.ds(pair * 128, 128)] = (part * factor).astype(BF16)
-
-    across.wait_recv()
-    v["ph_half"][...] = v["ph_in"][rows(base, 512)] + v["ph_core"][...]
-    scattered = pool.batch(v["ph_plane"])
-    for step in range(1, 16):
-        there = lax.rem(plane + step, 16)
-        scattered.add(
-            v["ph_half"].at[rows(there * 32, 32)], v["ph_plane"].at[step - 1], plane_device(step)
-        )
-
-    @pl.loop(0, 8)
-    def _(part):
-        where = rows(part * 256, 256)
-        v["series_t"][where] = v["series"][:, where].T
 
     own = pl.multiple_of(plane * 32, 32)
     v["proj_t"][...] = v["proj"][...].T
@@ -489,9 +505,9 @@
         for part in range(4):
             sums[0, pl.ds(part * 256 + first, 128)] = jnp.zeros((128, 128), F32)
 
-        @pl.loop(0, BLOCKS)
+        @pl.loop(0, ROWS // ATTENTION_BLOCK, unroll=2)
         def _(block):
-            where = rows(block * BLOCK, BLOCK)
+            where = rows(block * ATTENTION_BLOCK, ATTENTION_BLOCK)
             query = v["q_n"][where, lanes_of]
             grad = v["g_att"][where, lanes_of]
             scores = dot(query, v["key_in"][pair])

time: 105 us -> 105 us (level)
  no operation moved by 1% of the time
where the time goes in v6:
time: 105 us
  Pallas kernels  94.8 us (90%)
  local copies, waits for them, and re-layouts  9.1 us (9%)
    pallas_call x1, Pallas kernels, local(): pl.pallas_call(layer_kernel, out_shape=(jax.ShapeDtypeStruct((ROWS, WIDTH...  94.8 us
    unnamed x5, local copies, waits for them, and re-layouts  9.1 us

profile of v6, /device:TPU:1, one launch (start us, length us, event | category | flops | bytes accessed | tf_op | source)
XLA Modules:
  0.0 104.6 jit_solution(1479952459155567552)
XLA Ops:
  0.6 94.8 %shard_map.103 = (bf16[1024,512]{1,0:T(8,128)(2,1)}, f32[2048,512]{1,0:T(8,128)}, f32[4,512,512]{2,1,0:T(8,128)}) custom-call(bf16[1024,2048]{1,0:T(8,128)(2,1)} %refs_0_.1, bf16[2048,512]{1,0:T(8,128)(2,1)} %refs_1_.1, bf16[512,512]{1,0:T(8,128)(2,1)} %refs_2_.1, bf16[512,512]{1,0:T(8,128)(2,1)} %refs_3_.1, bf16[512,512]{1,0:T(8,128)(2,1)} %refs_4_.1, ...), custom_call_target="tpu_custom_call" | custom-call | tf_op jit(solution)/shard_map/pallas_call | solution.py:720
  95.5 2.3 %copy.14 = bf16[1024,512]{1,0:T(8,128)(2,1)} copy(bf16[1024,512]{1,0:T(8,128)(2,1)} %get-tuple-element.6) | data formatting | bytes 2097152
  97.7 0.0 copy-start
  97.7 4.8 %copy.15 = f32[2048,512]{1,0:T(8,128)} copy(f32[2048,512]{1,0:T(8,128)} %get-tuple-element.7) | data formatting | bytes 8388608
  102.6 0.0 copy-done
  102.6 2.0 %copy.16 = f32[4,512,512]{2,1,0:T(8,128)} copy(f32[4,512,512]{2,1,0:T(8,128)S(1)} %copy-done) | data formatting | bytes 8388608
Async XLA Ops:
  97.7 4.8 %copy-start = (f32[4,512,512]{2,1,0:T(8,128)S(1)}, f32[4,512,512]{2,1,0:T(8,128)}, u32[]{:S(2)}) copy-start(f32[4,512,512]{2,1,0:T(8,128)} %get-tuple-element.8) | copy-start | bytes 12582916

commit v7 on v6

--- a/solution.py
+++ b/solution.py
@@ -462,7 +462,6 @@
     passed.add(mine, mine, moved(here, c=1))
     passed.wait_recv()
     pool.drain([across, scattered])
-    sum_s.step2()
 
     loads["w_key"].wait()
     loads["w_value"].wait()
@@ -550,6 +549,7 @@
         sum_q[quad].core(2)
 
     attention(0)
+    sum_s.step2()
     attention(1)
     weight_grads(0)
     sum_s.step3()

time: 105 us -> 105 us (level)
  no operation moved by 1% of the time
where the time goes in v7:
time: 105 us
  Pallas kernels  94.8 us (90%)
  local copies, waits for them, and re-layouts  9.1 us (9%)
    pallas_call x1, Pallas kernels, local(): pl.pallas_call(layer_kernel, out_shape=(jax.ShapeDtypeStruct((ROWS, WIDTH...  94.8 us
    unnamed x5, local copies, waits for them, and re-layouts  9.1 us

profile of v7, /device:TPU:1, one launch (start us, length us, event | category | flops | bytes accessed | tf_op | source)
XLA Modules:
  0.0 104.5 jit_solution(12298130594554782718)
XLA Ops:
  0.6 94.8 %shard_map.103 = (bf16[1024,512]{1,0:T(8,128)(2,1)}, f32[2048,512]{1,0:T(8,128)}, f32[4,512,512]{2,1,0:T(8,128)}) custom-call(bf16[1024,2048]{1,0:T(8,128)(2,1)} %refs_0_.1, bf16[2048,512]{1,0:T(8,128)(2,1)} %refs_1_.1, bf16[512,512]{1,0:T(8,128)(2,1)} %refs_2_.1, bf16[512,512]{1,0:T(8,128)(2,1)} %refs_3_.1, bf16[512,512]{1,0:T(8,128)(2,1)} %refs_4_.1, ...), custom_call_target="tpu_custom_call" | custom-call | tf_op jit(solution)/shard_map/pallas_call | solution.py:720
  95.4 2.3 %copy.14 = bf16[1024,512]{1,0:T(8,128)(2,1)} copy(bf16[1024,512]{1,0:T(8,128)(2,1)} %get-tuple-element.6) | data formatting | bytes 2097152
  97.7 0.0 copy-start
  97.7 4.8 %copy.15 = f32[2048,512]{1,0:T(8,128)} copy(f32[2048,512]{1,0:T(8,128)} %get-tuple-element.7) | data formatting | bytes 8388608
  102.5 0.0 copy-done
  102.5 2.0 %copy.16 = f32[4,512,512]{2,1,0:T(8,128)} copy(f32[4,512,512]{2,1,0:T(8,128)S(1)} %copy-done) | data formatting | bytes 8388608
Async XLA Ops:
  97.7 4.8 %copy-start = (f32[4,512,512]{2,1,0:T(8,128)S(1)}, f32[4,512,512]{2,1,0:T(8,128)}, u32[]{:S(2)}) copy-start(f32[4,512,512]{2,1,0:T(8,128)} %get-tuple-element.8) | copy-start | bytes 12582916
